TPU v7x, 512 devices: a whole 4x4x16 slice. The times are simulated.
512 devices in a mesh: emb: 16 (over y_hi, x, core), dense: 32 (over y_lo, z).
Axes of the slice: x: 4, y: 4 (y_hi: 2, y_lo: 2; y = y_hi * 2 + y_lo), z: 16, core: 2. Of those that a mesh axis runs over, the one named last changes fastest.
Arguments:
- codes: int32 [16, 98304, 16], P('emb', 'dense'), may hold values from 0 to 255
- row_bag: int32 [16, 98304], P('emb', 'dense'), may hold values from 0 to 255
- codebook: bfloat16 [16, 256, 128], P('emb'), may hold values from -3 to 3
- w_in: bfloat16 [2048, 4096], P('emb'), may hold values from -0.125 to 0.125
- w_out: float32 [4096], replicated, may hold values from -0.09375 to 0.09375
- labels: float32 [8192], P('dense'), may hold values from 0 to 1
Outputs:
- grad_codebook: float32 [16, 256, 128], P('emb')
- grad_w_in: float32 [2048, 4096], P('emb')
- grad_w_out: float32 [4096], replicated
Inputs may be any that keep to these rules, and one draw needn't show every extreme that they name: `row_bag`: bags are ragged and may be empty.
All inputs are finite; a program needn't handle non-finite values.
Results may differ from a plain program's by a relative error of at most 0.0025.
Values may be sent and summed in bfloat16 or wider, within the bound.
A program may use at most 64 MiB of HBM per device.

v0:
```python
import jax
import jax.numpy as jnp
from jax import lax
from jax.sharding import PartitionSpec as P

D_FIELD = 128
SUB = 16
CENT = 256


block_rows = 256


def silu_slope(value):
    gate = jax.nn.sigmoid(value)
    return gate + value * gate * (1.0 - gate)


def body(codes, row_bag, codebook, w_in, w_out, labels):
    samp = labels.shape[0]
    rows = codes.shape[1]
    parts = lax.axis_size("emb")
    place = lax.axis_index("emb")
    sub_width = D_FIELD // SUB
    table = codebook[0].reshape(CENT, SUB, sub_width)
    code_blocks = codes[0].reshape(rows // block_rows, block_rows, SUB)
    bag_blocks = row_bag[0].reshape(rows // block_rows, block_rows)
    centroid_ids = jnp.arange(CENT, dtype=jnp.int32)
    sample_ids = jnp.arange(samp, dtype=jnp.int32)

    def pool_block(total, block):
        code_blk, bag_blk = block
        picks = (code_blk[:, :, None] == centroid_ids).astype(jnp.bfloat16)
        decoded = jnp.einsum("rmk,kmc->rmc", picks, table, preferred_element_type=jnp.float32)
        decoded = decoded.astype(jnp.bfloat16).reshape(block_rows, D_FIELD)
        members = (bag_blk[:, None] == sample_ids).astype(jnp.bfloat16)
        summed = lax.dot_general(
            members, decoded, (((0,), (0,)), ((), ())), preferred_element_type=jnp.float32
        )
        return (total + summed, None)

    pooled, _ = lax.scan(
        pool_block, jnp.zeros((samp, D_FIELD), jnp.float32), (code_blocks, bag_blocks)
    )
    pooled = pooled.astype(jnp.bfloat16)
    share = samp // parts
    pre = lax.psum_scatter(
        jnp.dot(pooled, w_in, preferred_element_type=jnp.float32),
        "emb",
        scatter_dimension=0,
        tiled=True,
    )
    act = jax.nn.silu(pre)
    logit = jnp.dot(act, w_out, precision=lax.Precision.HIGHEST)
    mine = lax.dynamic_slice_in_dim(labels, place * share, share, 0)
    slope = jax.nn.sigmoid(logit) - mine
    grad_hidden = (slope[:, None] * w_out[None, :] * silu_slope(pre)).astype(jnp.bfloat16)
    head_part = jnp.dot(slope, act, precision=lax.Precision.HIGHEST)
    piece = lax.all_gather(grad_hidden, "emb", axis=0, tiled=True)
    pool_rows = lax.dot_general(
        piece, w_in, (((1,), (1,)), ((), ())), preferred_element_type=jnp.float32
    )
    grad_weight = lax.dot_general(
        pooled, piece, (((0,), (0,)), ((), ())), preferred_element_type=jnp.float32
    )
    grad_pool, grad_weight = (pool_rows, grad_weight)
    grad_pool = grad_pool.astype(jnp.bfloat16)

    def table_block(total, block):
        code_blk, bag_blk = block
        picks = (code_blk[:, :, None] == centroid_ids).astype(jnp.bfloat16)
        members = (bag_blk[:, None] == sample_ids).astype(jnp.bfloat16)
        rows_grad = jnp.dot(members, grad_pool, preferred_element_type=jnp.float32)
        rows_grad = rows_grad.astype(jnp.bfloat16).reshape(block_rows, SUB, sub_width)
        return (
            total
            + jnp.einsum("rmk,rmc->kmc", picks, rows_grad, preferred_element_type=jnp.float32),
            None,
        )

    grad_table, _ = lax.scan(
        table_block, jnp.zeros((CENT, SUB, sub_width), jnp.float32), (code_blocks, bag_blocks)
    )
    grad_weight, grad_table, head_part = lax.psum(
        (grad_weight, grad_table.reshape(CENT, D_FIELD), head_part), "dense"
    )
    grad_head = lax.psum(head_part, "emb")
    return (grad_table[None], grad_weight, grad_head)


def solution(mesh):
    in_specs = (
        P("emb", "dense", None),
        P("emb", "dense"),
        P("emb", None, None),
        P("emb", None),
        P(),
        P("dense"),
    )
    out_specs = (P("emb", None, None), P("emb", None), P())
    return jax.shard_map(body, mesh=mesh, in_specs=in_specs, out_specs=out_specs, check_vma=False)
```

profile of v0, /device:TPU:6, one launch (start us, length us, event | category | flops | bytes accessed | tf_op | source)
XLA Modules:
  0.0 527.1 jit_solution(9545318869872072603)
XLA Ops:
  7.2 0.0 reduce-scatter.2.cloned.1.call-start
  7.2 1.1 reshape_squeeze.10
  8.3 0.1 copy.12
  8.4 0.5 broadcast.29
  8.9 1.4 reduce.3
  10.3 0.9 copy.11
  11.3 12.8 %while.26 = (s32[]{:T(128)}, f32[256,128]{1,0:T(8,128)S(1)}, s32[12,256]{1,0:T(8,128)S(1)}, s32[12,256,16]{1,2,0:T(8,128)S(1)}, bf16[256,16,8]{0,2,1:T(8,128)(2,1)S(1)}, /*index=5*/s32[]{:T(128)}, s32[]{:T(128)}) while((s32[]{:T(128)}, f32[256,128]{1,0:T(8,128)S(1)}, s32[12,256]{1,0:T(8,128)S(1)}, ...), condition=%wide.region_1.2_spmd.clone.clone, body=%wide.region_0.1_spmd.clone.clone.sunk | while | flops 34832384 | bytes 379999 | solution.py:42
  11.3 1.0 convolution_add_fusion.2
  12.4 1.0 convolution_add_fusion.2
  13.5 1.0 convolution_add_fusion.2
  14.5 1.0 convolution_add_fusion.2
  15.6 1.0 convolution_add_fusion.2
  16.7 1.0 convolution_add_fusion.2
  17.7 1.0 convolution_add_fusion.2
  18.8 1.0 convolution_add_fusion.2
  19.9 1.0 convolution_add_fusion.2
  20.9 1.0 convolution_add_fusion.2
  22.0 1.0 convolution_add_fusion.2
  23.1 1.0 convolution_add_fusion.2
  24.1 2.6 fusion.26
  26.8 0.0 reduce-scatter.2.cloned.1.call-update
  26.8 0.0 all-gather.2.cloned.1.call-start
  26.8 107.8 %reduce-scatter.2.cloned.1.call-done = f32[16,4096]{1,0:T(8,128)} async-done(((f32[256,4096]{1,0:T(8,128)}), f32[16,4096]{1,0:T(8,128)}) %reduce-scatter.2.cloned.1.call-update) | async-done | bytes 262160 | tf_op jit(solution)/shard_map/reduce_scatter | solution.py:47
  134.7 1.4 fusion.22
  136.0 0.0 copy-start.5
  136.1 0.5 copy-done.5
  136.6 1.7 multiply_convert_fusion
  138.3 0.0 all-gather.2.cloned.1.call-update
  138.4 0.0 all-reduce.3.cloned.1.call-start
  138.4 63.4 %all-gather.2.cloned.1.call-done = bf16[256,4096]{1,0:T(8,128)(2,1)} async-done(((bf16[16,4096]{1,0:T(8,128)(2,1)}), bf16[256,4096]{1,0:T(8,128)(2,1)}) %all-gather.2.cloned.1.call-update) | async-done | bytes 2097168 | tf_op jit(solution)/shard_map/all_gather | solution.py:59
  201.8 2.4 convolution_convert_fusion.1
  204.2 45.1 %while.27 = (s32[]{:T(128)}, f32[256,16,8]{0,2,1:T(8,128)}, s32[12,256]{1,0:T(8,128)}, bf16[256,128]{1,0:T(8,128)(2,1)S(1)}, s32[12,256,16]{1,2,0:T(8,128)S(1)}, /*index=5*/s32[]{:T(128)}, s32[]{:T(128)}) while((s32[]{:T(128)}, f32[256,16,8]{0,2,1:T(8,128)}, s32[12,256]{1,0:T(8,128)}, bf16[256,128]{1,0:T(8,128)(2,1)S(1)}, ...), condition=%wide.region_4.5_spmd.clone.clone, body=%wide.region_3.4_spmd.clone.clone.sunk | while | flops 34766848 | bytes 379999 | solution.py:81
  204.3 1.3 constant_dynamic-slice_fusion.5
  205.5 2.3 fusion.46
  207.8 1.3 constant_dynamic-slice_fusion.5
  209.1 2.5 fusion.46
  211.6 1.3 constant_dynamic-slice_fusion.5
  212.9 2.5 fusion.46
  215.4 1.3 constant_dynamic-slice_fusion.5
  216.6 2.5 fusion.46
  219.1 1.3 constant_dynamic-slice_fusion.5
  220.4 2.5 fusion.46
  222.9 1.3 constant_dynamic-slice_fusion.5
  224.2 2.5 fusion.46
  226.7 1.3 constant_dynamic-slice_fusion.5
  227.9 2.5 fusion.46
  230.5 1.3 constant_dynamic-slice_fusion.5
  231.7 2.5 fusion.46
  234.2 1.3 constant_dynamic-slice_fusion.5
  235.5 2.5 fusion.46
  238.0 1.3 constant_dynamic-slice_fusion.5
  239.3 2.5 fusion.46
  241.8 1.3 constant_dynamic-slice_fusion.5
  243.0 2.5 fusion.46
  245.6 1.3 constant_dynamic-slice_fusion.5
  246.8 2.5 fusion.46
  249.3 1.8 fusion.24
  251.2 0.9 copy-done.2
  252.1 0.3 fusion.28
  252.4 122.4 %psum.30 = f32[4096]{0:T(1024)S(1)} all-reduce(f32[4096]{0:T(1024)S(1)} %bitcast.71), channel_id=1, replica_groups=mesh['emb'=16,'dense'=32] {'dense'}, use_global_device_ids=true, to_apply=%region_7.8 | all-reduce | flops 4096 | bytes 32768 | tf_op jit(solution)/shard_map/psum | solution.py:84
  374.8 58.4 %psum.31 = f32[4096]{0:T(1024)} all-reduce(f32[4096]{0:T(1024)S(1)} %psum.30), channel_id=1, replica_groups=mesh['emb'=16,'dense'=32] {'emb'}, use_global_device_ids=true, to_apply=%region_8.9 | all-reduce | flops 4096 | bytes 32768 | tf_op jit(solution)/shard_map/psum | solution.py:87
  433.2 82.6 %all-reduce.3.cloned.1.call-done = (f32[1,256,128]{1,2,0:T(8,128)}, f32[128,4096]{1,0:T(8,128)}) async-done(((f32[1,256,128]{1,2,0:T(8,128)}, f32[128,4096]{1,0:T(8,128)}), (f32[1,256,128]{1,2,0:T(8,128)}, f32[128,4096]{1,0:T(8,128)})) %all-reduce.3.cloned.1.call-update) | async-done | bytes 2228240 | tf_op jit(solution)/shard_map/psum | solution.py:84
  515.8 1.7 copy.14
  517.4 3.1 copy.29
  (53 shorter events, 0.3 us)
Async XLA Ops:
  7.2 16.9 %copy-start = (bf16[128,4096]{1,0:T(8,128)(2,1)S(1)}, bf16[128,4096]{1,0:T(8,128)(2,1)}, u32[]{:S(2)}) copy-start(bf16[128,4096]{1,0:T(8,128)(2,1)} %param.13) | copy-start | bytes 3145732
  7.2 127.5 %reduce-scatter.2.cloned.1.call-start = ((), (), s32[]{:S(2)}) async-start(), calls=%async_computation.1 | async-start | bytes 4456448 | tf_op jit(solution)/shard_map/reduce_scatter | solution.py:47
  24.1 2.7 copy-start.3
  26.7 107.9 %copy-start.4 = (f32[4096]{0:T(1024)S(1)}, f32[4096]{0:T(1024)}, u32[]{:S(2)}) copy-start(f32[4096]{0:T(1024)} %param.14) | copy-start | bytes 49156
  26.8 107.9 %copy-start.7 = (f32[256]{0:T(256)S(1)}, f32[256]{0:T(256)}, u32[]{:S(2)}) copy-start(f32[256]{0:T(256)} %param.15) | copy-start | bytes 3076
  26.8 175.0 %all-gather.2.cloned.1.call-start = ((), (), s32[]{:S(2)}) async-start(), calls=%async_computation.2 | async-start | bytes 2228224 | tf_op jit(solution)/shard_map/all_gather | solution.py:59
  136.0 0.6 copy-start.5
  138.4 377.4 %all-reduce.3.cloned.1.call-start = ((), (), s32[]{:S(2)}) async-start(), calls=%async_computation.3 | async-start | bytes 4456448 | tf_op jit(solution)/shard_map/psum | solution.py:84
  201.8 47.5 %copy-start.1 = (bf16[256,4096]{1,0:T(8,128)(2,1)S(1)}, bf16[256,4096]{1,0:T(8,128)(2,1)}, u32[]{:S(2)}) copy-start(bf16[256,4096]{1,0:T(8,128)(2,1)} %all-gather.2.cloned.1.call-done) | copy-start | bytes 6291460
  251.1 0.9 copy-start.2
  251.1 1.0 copy-start.6
Sparse Core Ops, SparseCore 0:
  26.9 107.7 reduce-scatter.1
  139.1 62.6 all-gather.1
  251.3 264.4 all-reduce.2
where the time goes:
time: 528 us; the launch traced here: 527 us
  waiting for transfers between devices  254 us (48%)
  blocking collectives  181 us (34%)
  matrix products  50.5 us (10%)
  local copies, waits for them, and re-layouts  24.4 us (5%)
  between operations  13.9 us (3%)
    psum x1, blocking collectives, body(): lax.psum((grad_weight, grad_table.reshape(CENT, D_FIELD), head_part), 'de...  122 us
    reduce_scatter x1, waiting for transfers between devices, body(): lax.psum_scatter(jnp.dot(pooled, w_in, preferred_element_type=jnp.float32...  108 us
    psum x1, waiting for transfers between devices, body(): lax.psum((grad_weight, grad_table.reshape(CENT, D_FIELD), head_part), 'de...  82.6 us
    all_gather x1, waiting for transfers between devices, body(): piece = lax.all_gather(grad_hidden, 'emb', axis=0, tiled=True)  63.4 us
    psum x1, blocking collectives, body(): grad_head = lax.psum(head_part, 'emb')  58.4 us
    dot_general x12, matrix products, table_block(): jnp.einsum('rmk,rmc->kmc', picks, rows_grad, preferred_element_type=jnp.f...  29.9 us
    dynamic_slice x24, local copies, waits for them, and re-layouts, body(): lax.scan(pool_block, jnp.zeros((samp, D_FIELD), jnp.float32), (code_block...  15.3 us
    dot_general x12, matrix products, pool_block(): lax.dot_general(members, decoded, (((0,), (0,)), ((), ())), preferred_ele...  12 us
  transfers between devices with their start and end apart: 3, of which 3 were waited for; matrix products, arithmetic and copies ran while one was open for 0% of the time, Pallas kernels for 0%

commit v1 on v0

v1 whole, which is shorter than its diff:
```python
import functools

import jax
import jax.numpy as jnp
from jax import lax
from jax.experimental import pallas as pl
from jax.experimental.pallas import tpu as pltpu
from jax.sharding import PartitionSpec as P

D_FIELD = 128
SUB = 16
SUBW = 8
CENT = 256
EMB = 16
DENSE = 32
ZED = 16
SAMP = 256
WIDE = 256
HID = 4096
F32 = jnp.float32
BF16 = jnp.bfloat16
NT = (((1,), (1,)), ((), ()))
MESH = pl.DeviceIdType.MESH
BLOCK = 144


def pool_kernel(codes, bag, table, pooled, low, high, members):
    rows = codes.shape[1]

    def onehot(row):
        ids = lax.broadcasted_iota(jnp.int32, (CENT, rows), 0)
        return jnp.where(row == ids, 1.0, 0.0).astype(BF16)

    members[...] = onehot(bag[...])

    def step(m, carry):
        count = lax.dot_general(onehot(codes[pl.ds(m, 1), :]), members[...], NT, preferred_element_type=F32)
        upper = jnp.floor(count * (1.0 / 256.0))
        lower = count - upper * 256.0
        place = pl.ds(pl.multiple_of(m * CENT, CENT), CENT)
        low[place, :] = lower.astype(BF16)
        high[place, :] = upper.astype(BF16)
        part = table[pl.ds(pl.multiple_of(m * SUBW, SUBW), SUBW), :].astype(BF16)
        pooled[pl.ds(pl.multiple_of(m * SUBW, SUBW), SUBW), :] = jnp.dot(
            part, lower.astype(BF16), preferred_element_type=F32
        ) + 256.0 * jnp.dot(part, upper.astype(BF16), preferred_element_type=F32)
        return carry

    lax.fori_loop(0, SUB, step, 0)


def pool(codes, bag, table):
    vmem = pl.BlockSpec(memory_space=pltpu.VMEM)
    counts = jax.ShapeDtypeStruct((SUB * CENT, SAMP), BF16)
    return pl.pallas_call(
        pool_kernel,
        out_shape=(jax.ShapeDtypeStruct((D_FIELD, SAMP), F32), counts, counts),
        in_specs=[vmem] * 3,
        out_specs=(vmem,) * 3,
        scratch_shapes=[pltpu.VMEM((SAMP, codes.shape[1]), BF16)],
        compiler_params=pltpu.CompilerParams(vmem_limit_bytes=40 << 20),
        name="pool",
    )(codes, bag, table)


def step_kernel(
    pooled, low, high, w_in, w_out, labels, out,
    w_cols, w_turned, fields, fields32, turned, logits, heads, pool_out, pool_in,
    y_out, y_in, mine, near_out, near_in, acc, far_out, far_in, red, cols,
    tab, tab_y, tab_near, tab_far,
    local, w_s, w_r, f_s, f_r, sib_s, sib_r, lg_s, lg_r, hd_s, hd_r, gp_s, gp_r,
    y_s, y_r, n_s, n_r, fr_s, fr_r, a_s, a_r,
    ty_s, ty_r, tn_s, tn_r, tf_s, tf_r, of_s, of_r, on_s, on_r, oy_s, oy_r,
):
    e = lax.axis_index("emb")
    g = lax.axis_index("dense")
    y = g // ZED
    z = lax.rem(g, ZED)
    zq = z // 4
    zr = lax.rem(z, 4)
    sib = e + 1 - 2 * lax.rem(e, 2)
    other = 1 - y

    def emb_at(i):
        return lax.rem(e + i, EMB)

    def emb_from(i):
        return lax.rem(e + EMB - i, EMB)

    def z_at(off):
        return (e, y * ZED + lax.rem(z + off + ZED, ZED))

    def send(src, dst, ss, rs, to):
        return pltpu.make_async_remote_copy(
            src_ref=src, dst_ref=dst, send_sem=ss, recv_sem=rs, device_id=to, device_id_type=MESH
        )

    def loop(lo, hi, body):
        def step(i, carry):
            body(i)
            return carry

        lax.fori_loop(lo, hi, step, 0)

    y_mate = (e, other * ZED + z)
    barrier = pltpu.get_barrier_semaphore()
    loop(1, EMB, lambda i: pl.semaphore_signal(barrier, inc=1, device_id=(emb_at(i), g), device_id_type=MESH))
    for off in (1, -1, 2, -2, 4, -4, 8):
        pl.semaphore_signal(barrier, inc=1, device_id=z_at(off), device_id_type=MESH)
    pl.semaphore_signal(barrier, inc=1, device_id=y_mate, device_id_type=MESH)
    pl.semaphore_wait(barrier, EMB - 1 + 8)

    def w_copy(i):
        cols_of = pl.ds(pl.multiple_of(emb_at(i) * WIDE, WIDE), WIDE)
        return send(w_in.at[:, cols_of], w_cols.at[e], w_s.at[i], w_r.at[i], (emb_at(i), g))

    def f_copy(i):
        return send(fields.at[e], fields.at[e], f_s.at[i], f_r.at[i], (emb_at(2 * i), g))

    def sib_copy(i):
        f = lax.rem(e + 2 * EMB - 2 * i, EMB)
        return send(fields.at[f], fields.at[f], sib_s.at[i], sib_r.at[i], (sib, g))

    fields[e] = pooled[...].astype(BF16)
    loop(1, 8, lambda i: f_copy(i).start())
    sib_copy(0).start()
    loop(1, EMB, lambda i: w_copy(i).start())
    own_w = pltpu.make_async_copy(
        w_in.at[:, pl.ds(pl.multiple_of(e * WIDE, WIDE), WIDE)], w_cols.at[e], local.at[0]
    )
    own_w.start()

    def forward(i):
        f_copy(i).wait_recv()
        sib_copy(i).start()

    loop(1, 8, forward)
    loop(0, 8, lambda i: sib_copy(i).wait_recv())
    own_w.wait()
    loop(1, EMB, lambda i: w_copy(i).wait_recv())
    for f in range(EMB):
        w_turned[:, f * D_FIELD : (f + 1) * D_FIELD] = w_cols[f].T

    pre = jnp.dot(w_turned[...], fields[...].reshape(EMB * D_FIELD, SAMP), preferred_element_type=F32)
    gate = jax.nn.sigmoid(pre)
    act = pre * gate
    w_row = jnp.concatenate([w_out[pl.ds(2 * e, 1), :], w_out[pl.ds(2 * e + 1, 1), :]], axis=1)
    w_rows = jnp.broadcast_to(w_row, (8, WIDE))
    logits[e] = jnp.dot(w_rows, act, precision=lax.Precision.HIGHEST, preferred_element_type=F32)

    def lg_copy(i):
        return send(logits.at[e], logits.at[e], lg_s.at[i], lg_r.at[i], (emb_at(i), g))

    loop(1, EMB, lambda i: lg_copy(i).start())

    for f in range(EMB):
        fields32[:, f] = fields[f].astype(F32).reshape(16, 8, SAMP)
    for c in range(4):
        for a in range(4):
            turned[c, a * 128 : (a + 1) * 128] = fields32[a * 4 + c].reshape(128, SAMP).astype(BF16)
    slant = gate + pre * gate * (1.0 - gate)
    w_left = jnp.broadcast_to(w_row[:, :128], (128, 128)).T
    w_right = jnp.broadcast_to(w_row[:, 128:], (128, 128)).T
    w_tall = jnp.concatenate([w_left, w_right], axis=0)
    w_tall = jnp.concatenate([w_tall, w_tall], axis=1)

    loop(1, EMB, lambda i: lg_copy(i).wait_recv())
    logit = logits[0]
    for f in range(1, EMB):
        logit = logit + logits[f]
    slope = jax.nn.sigmoid(logit) - labels[...]
    grad = (slope[:1] * w_tall * slant).astype(BF16)
    halves = (grad[:128], grad[128:])

    head = lax.dot_general(slope, act, NT, precision=lax.Precision.HIGHEST, preferred_element_type=F32)
    heads[e] = jnp.concatenate([head[:1, :128], head[:1, 128:], jnp.zeros((6, 128), F32)], axis=0)

    def hd_copy(i):
        return send(heads.at[e], heads.at[e], hd_s.at[i], hd_r.at[i], (emb_at(i), g))

    loop(1, EMB, lambda i: hd_copy(i).start())

    def gp_copy(i):
        return send(pool_out.at[emb_at(i)], pool_in.at[e], gp_s.at[i], gp_r.at[i], (emb_at(i), g))

    def gp_part(i):
        f = emb_at(i)
        pool_out[f] = jnp.dot(w_cols[f], grad, preferred_element_type=F32)

    def gp_start(i):
        gp_part(i)
        gp_copy(i).start()

    loop(1, EMB, gp_start)
    gp_part(0)
    pool_in[e] = pool_out[e]

    def grad_half(c, half):
        rhs = jnp.where(half == 0, halves[0], halves[1])
        return lax.dot_general(turned[c], rhs, NT, preferred_element_type=F32)

    def y_copy(k, c):
        return send(y_out.at[c], y_in.at[c], y_s.at[k], y_r.at[k], y_mate)

    near = (2, 1, -1)
    order = [lax.rem(z + off + 4, 4) for off in near] + [zr]
    for k, c in enumerate(order):
        y_out[c] = grad_half(c, other).astype(BF16)
        y_copy(k, c).start()
    for k, c in enumerate(order):
        mine[c] = grad_half(c, y)

    def near_copy(k):
        return send(near_out.at[k], near_in.at[k], n_s.at[k], n_r.at[k], z_at(near[k]))

    for k in range(3):
        c = order[k]
        y_copy(k, c).wait_recv()
        near_out[k] = mine[c] + y_in[c].astype(F32)
        near_copy(k).start()
    y_copy(3, zr).wait_recv()
    acc[...] = (mine[zr] + y_in[zr].astype(F32)).reshape(4, 128, 128)

    loop(1, EMB, lambda i: gp_copy(i).wait_recv())
    total = pool_in[0]
    for f in range(1, EMB):
        total = total + pool_in[f]
    grad_pool = total.astype(BF16)
    parts = []
    for m in range(SUB):
        rows = grad_pool[m * SUBW : (m + 1) * SUBW]
        span = slice(m * CENT, (m + 1) * CENT)
        parts.append(
            lax.dot_general(rows, low[span, :], NT, preferred_element_type=F32)
            + 256.0 * lax.dot_general(rows, high[span, :], NT, preferred_element_type=F32)
        )
    table = jnp.concatenate(parts, axis=0).T
    loop(1, EMB, lambda i: hd_copy(i).wait_recv())
    for yy in range(2):
        for zz in range(ZED):
            gg = yy * ZED + zz
            tab[yy, zz % 4, zz // 4, :8] = table[gg * 8 : gg * 8 + 8]
            tab[yy, zz % 4, zz // 4, 8:] = jnp.concatenate(
                [heads[gg // 2, gg % 2 : gg % 2 + 1], jnp.zeros((7, 128), F32)], axis=0
            )
    ty_copy = send(tab.at[other], tab_y, ty_s, ty_r, y_mate)
    ty_copy.start()

    for k in range(3):
        near_copy(k).wait_recv()
        acc[...] = acc[...] + near_in[k].reshape(4, 128, 128)

    def far_copy(m):
        return send(far_out.at[m - 1], far_in.at[m - 1], fr_s.at[m - 1], fr_r.at[m - 1], z_at(4 * m))

    for m in range(1, 4):
        far_out[m - 1] = acc[lax.rem(zq + m, 4)]
        far_copy(m).start()

    ty_copy.wait_recv()
    tab[y] = tab[y] + tab_y[...]

    def tn_copy(k):
        return send(tab.at[y, order[k]], tab_near.at[k], tn_s.at[k], tn_r.at[k], z_at(near[k]))

    for k in range(3):
        tn_copy(k).start()

    whole = acc[zq]
    for m in range(1, 4):
        far_copy(m).wait_recv()
        whole = whole + far_in[m - 1]
    red[...] = whole.reshape(EMB, 8, 128)

    def a_copy(i):
        return send(red.at[emb_at(i)], cols.at[e], a_s.at[i], a_r.at[i], (emb_at(i), g))

    loop(1, EMB, lambda i: a_copy(i).start())
    cols[e] = red[e]

    for k in range(3):
        tn_copy(k).wait_recv()
    tab_sum = tab[y, zr] + tab_near[0] + tab_near[1] + tab_near[2]
    tab[y, zr] = tab_sum

    def tf_copy(m):
        return send(
            tab.at[y, zr, lax.rem(zq + m, 4)], tab_far.at[m - 1], tf_s.at[m - 1], tf_r.at[m - 1], z_at(4 * m)
        )

    for m in range(1, 4):
        tf_copy(m).start()
    for m in range(1, 4):
        tf_copy(m).wait_recv()
    tab_whole = tab[y, zr, zq] + tab_far[0] + tab_far[1] + tab_far[2]
    out[y, zr, zq, 128:] = tab_whole
    loop(1, EMB, lambda i: a_copy(i).wait_recv())
    out[y, zr, zq, :128] = cols[...].reshape(128, 128)

    def block(off, m):
        src = lax.rem(z + 2 * ZED - off - 4 * m, ZED)
        return out.at[y, lax.rem(src, 4), src // 4]

    def of_copy(m):
        return send(block(0, 0), block(0, 0), of_s.at[m - 1], of_r.at[m - 1], z_at(4 * m))

    def of_wait(m):
        send(block(0, m), block(0, m), of_s.at[m - 1], of_r.at[m - 1], z_at(4 * m)).wait_recv()

    ways = (1, -1, 2)

    def on_copy(k, m):
        return send(block(0, m), block(0, m), on_s.at[k, m], on_r.at[k, m], z_at(ways[k]))

    def on_wait(k, m):
        got = block(ways[k], m)
        send(got, got, on_s.at[k, m], on_r.at[k, m], z_at(ways[k])).wait_recv()

    def oy_copy(k, m):
        got = block(0 if k == 0 else ways[k - 1], m)
        return send(got, got, oy_s.at[k, m], oy_r.at[k, m], y_mate)

    def oy_wait(k, m):
        src = lax.rem(z + 2 * ZED - (0 if k == 0 else ways[k - 1]) - 4 * m, ZED)
        got = out.at[other, lax.rem(src, 4), src // 4]
        send(got, got, oy_s.at[k, m], oy_r.at[k, m], y_mate).wait_recv()

    for m in range(1, 4):
        of_copy(m).start()
    for m in range(4):
        if m:
            of_wait(m)
        for k in range(3):
            on_copy(k, m).start()
        oy_copy(0, m).start()
    for m in range(4):
        for k in range(3):
            on_wait(k, m)
            oy_copy(k + 1, m).start()
    for m in range(4):
        for k in range(4):
            oy_wait(k, m)

    loop(1, 8, lambda i: f_copy(i).wait_send())
    loop(0, 8, lambda i: sib_copy(i).wait_send())

    def sent(i):
        w_copy(i).wait_send()
        lg_copy(i).wait_send()
        hd_copy(i).wait_send()
        gp_copy(i).wait_send()
        a_copy(i).wait_send()

    loop(1, EMB, sent)
    for k, c in enumerate(order):
        y_copy(k, c).wait_send()
    ty_copy.wait_send()
    for k in range(3):
        near_copy(k).wait_send()
        tn_copy(k).wait_send()
    for m in range(1, 4):
        far_copy(m).wait_send()
        tf_copy(m).wait_send()
        of_copy(m).wait_send()
    for m in range(4):
        for k in range(3):
            on_copy(k, m).wait_send()
        for k in range(4):
            oy_copy(k, m).wait_send()


def train(pooled, low, high, w_in, w_out, labels):
    vmem = pl.BlockSpec(memory_space=pltpu.VMEM)
    V, D = pltpu.VMEM, pltpu.SemaphoreType.DMA
    scratch = [
        V((EMB, D_FIELD, WIDE), BF16),
        V((WIDE, EMB * D_FIELD), BF16),
        V((EMB, D_FIELD, SAMP), BF16),
        V((16, EMB, 8, SAMP), F32),
        V((4, 512, SAMP), BF16),
        V((EMB, 8, SAMP), F32),
        V((EMB, 8, 128), F32),
        V((EMB, D_FIELD, SAMP), F32),
        V((EMB, D_FIELD, SAMP), F32),
        V((4, 512, 128), BF16),
        V((4, 512, 128), BF16),
        V((4, 512, 128), F32),
        V((3, 512, 128), F32),
        V((3, 512, 128), F32),
        V((4, 128, 128), F32),
        V((3, 128, 128), F32),
        V((3, 128, 128), F32),
        V((EMB, 8, 128), F32),
        V((EMB, 8, 128), F32),
        V((2, 4, 4, 16, 128), F32),
        V((4, 4, 16, 128), F32),
        V((3, 4, 16, 128), F32),
        V((3, 16, 128), F32),
        D((1,)),
    ]
    sems = [(16,), (8,), (8,), (16,), (16,), (16,), (4,), (3,), (3,), (16,), (), (3,), (3,), (3,), (3, 4), (4, 4)]
    for shape in sems:
        scratch += [D(shape), D(shape)] if shape else [D, D]
    return pl.pallas_call(
        step_kernel,
        out_shape=jax.ShapeDtypeStruct((2, 4, 4, BLOCK, 128), F32),
        in_specs=[vmem, vmem, vmem, pl.BlockSpec(memory_space=pl.ANY), vmem, vmem],
        out_specs=vmem,
        scratch_shapes=scratch,
        compiler_params=pltpu.CompilerParams(
            collective_id=1, has_side_effects=True, vmem_limit_bytes=48 << 20
        ),
        name="train_step",
    )(pooled, low, high, w_in, w_out, labels)


def spread_kernel(gathered, weight, table, head):
    a = pl.program_id(0)
    for c in range(4):
        for yy in range(2):
            for f in range(EMB):
                spot = f * WIDE + yy * 128
                weight[c * 8 : c * 8 + 8, spot : spot + 128] = gathered[yy, c, 0, f * 8 : f * 8 + 8]
            tab = gathered[yy, c, 0, 128:]
            gg = yy * ZED + a * 4 + c
            table[pl.ds(pl.multiple_of(gg * 8, 8), 8), :] = tab[:8]
            head[pl.ds(gg, 1), :] = tab[8:9]


def spread(gathered):
    return pl.pallas_call(
        spread_kernel,
        grid=(4,),
        out_shape=(
            jax.ShapeDtypeStruct((D_FIELD, HID), F32),
            jax.ShapeDtypeStruct((CENT, D_FIELD), F32),
            jax.ShapeDtypeStruct((DENSE, 128), F32),
        ),
        in_specs=[pl.BlockSpec((2, 4, 1, BLOCK, 128), lambda i: (0, 0, i, 0, 0))],
        out_specs=(
            pl.BlockSpec((32, HID), lambda i: (i, 0)),
            pl.BlockSpec((CENT, D_FIELD), lambda i: (0, 0)),
            pl.BlockSpec((DENSE, 128), lambda i: (0, 0)),
        ),
        name="spread",
    )(gathered)


def body(codes, row_bag, codebook, w_in, w_out, labels):
    pooled, low, high = pool(codes[0].T, row_bag, codebook[0].T.astype(F32))
    gathered = train(pooled, low, high, w_in, w_out.reshape(32, 128), labels.reshape(1, SAMP))
    weight, table, head = spread(gathered)
    return table[None], weight, head.reshape(HID)


def solution(mesh):
    in_specs = (
        P("emb", "dense", None),
        P("emb", "dense"),
        P("emb", None, None),
        P("emb", None),
        P(),
        P("dense"),
    )
    out_specs = (P("emb", None, None), P("emb", None), P())
    return jax.shard_map(body, mesh=mesh, in_specs=in_specs, out_specs=out_specs, check_vma=False)
```

time: 528 us -> 181 us (0.34)
  waiting for transfers between devices: 254 us -> 0 us
  blocking collectives: 181 us -> 0 us
  Pallas kernels: 0 us -> 175 us
  matrix products: 50.5 us -> 0 us
  local copies, waits for them, and re-layouts: 24.4 us -> 5.2 us
  between operations: 13.9 us -> 0.67 us
    psum x2 -> x0, blocking collectives: 181 us -> none  [the longest x1 122 us: body(): lax.psum((grad_weight, grad_table.reshape(CENT, D_FIELD), head_part), 'de...]
    pallas_call x0 -> x3, Pallas kernels: none -> 175 us  [the longest x1 157 us: train(): pl.pallas_call(step_kernel, out_shape=jax.ShapeDtypeStruct((2, 4, 4, BLOC...]
    reduce_scatter x1 -> x0, waiting for transfers between devices: 108 us -> none  [body(): lax.psum_scatter(jnp.dot(pooled, w_in, preferred_element_type=jnp.float32...]
    psum x1 -> x0, waiting for transfers between devices: 82.6 us -> none  [body(): lax.psum((grad_weight, grad_table.reshape(CENT, D_FIELD), head_part), 'de...]
    all_gather x1 -> x0, waiting for transfers between devices: 63.4 us -> none  [body(): piece = lax.all_gather(grad_hidden, 'emb', axis=0, tiled=True)]
    dot_general x29 -> x0, matrix products: 50.5 us -> none  [the longest x12 29.9 us: table_block(): jnp.einsum('rmk,rmc->kmc', picks, rows_grad, preferred_element_type=jnp.f...]
    dynamic_slice x24 -> x0, local copies, waits for them, and re-layouts: 15.3 us -> none  [body(): lax.scan(pool_block, jnp.zeros((samp, D_FIELD), jnp.float32), (code_block...]
  transfers between devices with their start and end apart: 3 -> 0, of which waited for: 3 -> 0; matrix products, arithmetic and copies ran while one was open for 0% -> 0% of each run, Pallas kernels for 0% -> 0%
where the time goes in v1:
time: 181 us; the launch traced here: 180 us
  Pallas kernels  175 us (97%)
  local copies, waits for them, and re-layouts  5.2 us (3%)
    pallas_call x1, Pallas kernels, train(): pl.pallas_call(step_kernel, out_shape=jax.ShapeDtypeStruct((2, 4, 4, BLOC...  157 us
    pallas_call x1, Pallas kernels, pool(): pl.pallas_call(pool_kernel, out_shape=(jax.ShapeDtypeStruct((D_FIELD, SAM...  13.1 us
    unnamed x11, local copies, waits for them, and re-layouts  5.2 us
    pallas_call x1, Pallas kernels, spread(): pl.pallas_call(spread_kernel, grid=(4,), out_shape=(jax.ShapeDtypeStruct(...  3.89 us

profile of v1, /device:TPU:6, one launch (start us, length us, event | category | flops | bytes accessed | tf_op | source)
XLA Modules:
  0.0 180.4 jit_solution(10983768433322780664)
XLA Ops:
  0.6 0.9 copy.9
  1.6 0.0 copy-start.1
  1.6 0.9 copy-done.1
  2.5 0.0 copy-start.3
  2.5 0.7 copy-done.3
  3.2 13.1 %pool.1 = (f32[128,256]{1,0:T(8,128)S(1)}, bf16[4096,256]{1,0:T(8,128)(2,1)S(1)}, bf16[4096,256]{1,0:T(8,128)(2,1)S(1)}) custom-call(s32[16,3072]{1,0:T(8,128)S(1)} %bitcast.12, s32[1,3072]{1,0:T(1,128)S(1)} %copy-done.3, f32[128,256]{1,0:T(8,128)S(1)} %convert_bitcast_fusion.table), custom_call_target="tpu_custom_call" | custom-call | tf_op jit(solution)/shard_map/pool/pallas_call | solution.py:55
  16.4 0.0 copy-start
  16.4 1.2 copy-done
  17.6 0.0 copy-start.2
  17.6 0.7 copy-done.2
  18.3 0.0 copy-start.4
  18.3 0.7 copy-done.4
  19.0 157.5 %train_step.1.gathered = f32[2,4,4,144,128]{4,3,2,1,0:T(8,128)} custom-call(f32[128,256]{1,0:T(8,128)S(1)} %get-tuple-element.9.pooled, bf16[4096,256]{1,0:T(8,128)(2,1)S(1)} %get-tuple-element.10.low, bf16[4096,256]{1,0:T(8,128)(2,1)S(1)} %get-tuple-element.11.high, bf16[128,4096]{1,0:T(8,128)(2,1)S(1)} %copy-done, f32[32,128]{1,0:T(8,128)S(1)} %bitcast.13, ...), custom_call_target="tpu_custom_call" | custom-call | tf_op jit(solution)/shard_map/train_step/pallas_call | solution.py:404
  176.5 3.9 %spread.1 = (f32[128,4096]{1,0:T(8,128)}, f32[256,128]{1,0:T(8,128)}, f32[32,128]{1,0:T(8,128)}) custom-call(f32[2,4,4,144,128]{4,3,2,1,0:T(8,128)} %train_step.1.gathered), custom_call_target="tpu_custom_call" | custom-call | tf_op jit(solution)/shard_map/spread/pallas_call | solution.py:431
  (1 shorter events, 0.0 us)
Async XLA Ops:
  1.6 0.9 copy-start.1
  2.5 0.7 copy-start.3
  16.4 1.2 copy-start
  17.6 0.7 copy-start.2
  18.3 0.7 copy-start.4

commit v2 on v1

--- a/solution.py
+++ b/solution.py
@@ -19,56 +19,41 @@
 HID = 4096
 F32 = jnp.float32
 BF16 = jnp.bfloat16
+F8 = jnp.float8_e4m3fn
+I16 = jnp.int16
 NT = (((1,), (1,)), ((), ()))
 MESH = pl.DeviceIdType.MESH
-BLOCK = 144
-
-
-def pool_kernel(codes, bag, table, pooled, low, high, members):
-    rows = codes.shape[1]
-
-    def onehot(row):
-        ids = lax.broadcasted_iota(jnp.int32, (CENT, rows), 0)
-        return jnp.where(row == ids, 1.0, 0.0).astype(BF16)
-
-    members[...] = onehot(bag[...])
-
-    def step(m, carry):
-        count = lax.dot_general(onehot(codes[pl.ds(m, 1), :]), members[...], NT, preferred_element_type=F32)
-        upper = jnp.floor(count * (1.0 / 256.0))
-        lower = count - upper * 256.0
-        place = pl.ds(pl.multiple_of(m * CENT, CENT), CENT)
-        low[place, :] = lower.astype(BF16)
-        high[place, :] = upper.astype(BF16)
-        part = table[pl.ds(pl.multiple_of(m * SUBW, SUBW), SUBW), :].astype(BF16)
-        pooled[pl.ds(pl.multiple_of(m * SUBW, SUBW), SUBW), :] = jnp.dot(
-            part, lower.astype(BF16), preferred_element_type=F32
-        ) + 256.0 * jnp.dot(part, upper.astype(BF16), preferred_element_type=F32)
-        return carry
-
-    lax.fori_loop(0, SUB, step, 0)
-
-
-def pool(codes, bag, table):
-    vmem = pl.BlockSpec(memory_space=pltpu.VMEM)
-    counts = jax.ShapeDtypeStruct((SUB * CENT, SAMP), BF16)
-    return pl.pallas_call(
-        pool_kernel,
-        out_shape=(jax.ShapeDtypeStruct((D_FIELD, SAMP), F32), counts, counts),
-        in_specs=[vmem] * 3,
-        out_specs=(vmem,) * 3,
-        scratch_shapes=[pltpu.VMEM((SAMP, codes.shape[1]), BF16)],
-        compiler_params=pltpu.CompilerParams(vmem_limit_bytes=40 << 20),
-        name="pool",
-    )(codes, bag, table)
+BLOCK = 160
+GROUP = 4
+
+
+def encode(value):
+    top = jnp.maximum(jnp.max(jnp.abs(value), axis=0, keepdims=True), 1e-30)
+    power = jnp.ceil(jnp.log2(top) + 0.001)
+    coded = jnp.floor(value * jnp.exp2(15.0 - power) + 0.5)
+    return coded.astype(jnp.int32).astype(I16), power
+
+
+def tile_of(power):
+    return jnp.broadcast_to(power, (16, power.shape[1])).astype(jnp.int32).astype(I16)
+
+
+def number(coded):
+    return coded.astype(jnp.int32).astype(F32)
+
+
+def decode(coded, power):
+    return number(coded) * jnp.exp2(number(power)[:1] - 15.0)
 
 
 def step_kernel(
-    pooled, low, high, w_in, w_out, labels, out,
-    w_cols, w_turned, fields, fields32, turned, logits, heads, pool_out, pool_in,
+    codes_hbm, bag_hbm, book_hbm, w_in, w_out_hbm, labels_hbm, out,
+    codes, bag, book, w_out, labels, table_t, members, pooled, low, high,
+    w_cols, w_turned, fields, fields32, turned, logits, heads,
+    gp_own, gp_sib, gp_got, gp_out, gp_in,
     y_out, y_in, mine, near_out, near_in, acc, far_out, far_in, red, cols,
     tab, tab_y, tab_near, tab_far,
-    local, w_s, w_r, f_s, f_r, sib_s, sib_r, lg_s, lg_r, hd_s, hd_r, gp_s, gp_r,
+    local, w_s, w_r, f_s, f_r, sib_s, sib_r, lg_s, lg_r, hd_s, hd_r, gs_s, gs_r, gp_s, gp_r,
     y_s, y_r, n_s, n_r, fr_s, fr_r, a_s, a_r,
     ty_s, ty_r, tn_s, tn_r, tf_s, tf_r, of_s, of_r, on_s, on_r, oy_s, oy_r,
 ):
@@ -103,6 +88,15 @@
         lax.fori_loop(lo, hi, step, 0)
 
     y_mate = (e, other * ZED + z)
+    loads = [
+        pltpu.make_async_copy(src, dst, local.at[1 + i])
+        for i, (src, dst) in enumerate(
+            ((bag_hbm, bag), (codes_hbm, codes), (book_hbm, book), (w_out_hbm, w_out), (labels_hbm, labels))
+        )
+    ]
+    for load in loads:
+        load.start()
+    sent = []
     barrier = pltpu.get_barrier_semaphore()
     loop(1, EMB, lambda i: pl.semaphore_signal(barrier, inc=1, device_id=(emb_at(i), g), device_id_type=MESH))
     for off in (1, -1, 2, -2, 4, -4, 8):
@@ -114,30 +108,69 @@
         cols_of = pl.ds(pl.multiple_of(emb_at(i) * WIDE, WIDE), WIDE)
         return send(w_in.at[:, cols_of], w_cols.at[e], w_s.at[i], w_r.at[i], (emb_at(i), g))
 
-    def f_copy(i):
-        return send(fields.at[e], fields.at[e], f_s.at[i], f_r.at[i], (emb_at(2 * i), g))
-
-    def sib_copy(i):
+    def rows_of(f, h):
+        return fields.at[f, pl.ds(h * 64, 64)]
+
+    def f_copy(i, h):
+        return send(rows_of(e, h), rows_of(e, h), f_s.at[h, i], f_r.at[h, i], (emb_at(2 * i), g))
+
+    def sib_copy(i, h):
         f = lax.rem(e + 2 * EMB - 2 * i, EMB)
-        return send(fields.at[f], fields.at[f], sib_s.at[i], sib_r.at[i], (sib, g))
-
-    fields[e] = pooled[...].astype(BF16)
-    loop(1, 8, lambda i: f_copy(i).start())
-    sib_copy(0).start()
+        return send(rows_of(f, h), rows_of(f, h), sib_s.at[h, i], sib_r.at[h, i], (sib, g))
+
     loop(1, EMB, lambda i: w_copy(i).start())
+    sent.append(lambda: loop(1, EMB, lambda i: w_copy(i).wait_send()))
     own_w = pltpu.make_async_copy(
         w_in.at[:, pl.ds(pl.multiple_of(e * WIDE, WIDE), WIDE)], w_cols.at[e], local.at[0]
     )
     own_w.start()
 
-    def forward(i):
-        f_copy(i).wait_recv()
-        sib_copy(i).start()
-
-    loop(1, 8, forward)
-    loop(0, 8, lambda i: sib_copy(i).wait_recv())
+    def onehot(row):
+        ids = lax.broadcasted_iota(jnp.int32, (CENT, row.shape[1]), 0)
+        return jnp.where(row == ids, 1.0, 0.0).astype(F8)
+
+    for load in loads:
+        load.wait()
+    members[...] = onehot(bag[...])
+    table_t[...] = book[...].astype(F32).T
+
+    def count_step(step):
+        at = step * GROUP
+        picks = jnp.concatenate([onehot(codes[pl.ds(at + j, 1), :]) for j in range(GROUP)], axis=0)
+        count = lax.dot_general(picks, members[...], NT, preferred_element_type=F32)
+        upper = jnp.floor(count * (1.0 / 256.0))
+        lower = (count - upper * 256.0).astype(BF16)
+        upper = upper.astype(BF16)
+        place = pl.ds(pl.multiple_of(at * CENT, CENT * GROUP), CENT * GROUP)
+        low[place, :] = lower
+        high[place, :] = upper
+        rows = pl.ds(pl.multiple_of(at * SUBW, SUBW * GROUP), SUBW * GROUP)
+        part = table_t[rows, :].astype(BF16)
+        for j in range(GROUP):
+            mine_at = slice(j * SUBW, (j + 1) * SUBW)
+            span = slice(j * CENT, (j + 1) * CENT)
+            pooled[pl.ds(pl.multiple_of((at + j) * SUBW, SUBW), SUBW), :] = jnp.dot(
+                part[mine_at], lower[span], preferred_element_type=F32
+            ) + 256.0 * jnp.dot(part[mine_at], upper[span], preferred_element_type=F32)
+
+    for h in range(2):
+        loop(h * 2, h * 2 + 2, count_step)
+        fields[e, h * 64 : h * 64 + 64] = pooled[h * 64 : h * 64 + 64].astype(BF16)
+        loop(1, 8, lambda i: f_copy(i, h).start())
+        sib_copy(0, h).start()
+        sent.append(lambda h=h: loop(1, 8, lambda i: f_copy(i, h).wait_send()))
+        sent.append(lambda h=h: loop(0, 8, lambda i: sib_copy(i, h).wait_send()))
+
+    def forward(i, h):
+        f_copy(i, h).wait_recv()
+        sib_copy(i, h).start()
+
+    for h in range(2):
+        loop(1, 8, lambda i: forward(i, h))
     own_w.wait()
     loop(1, EMB, lambda i: w_copy(i).wait_recv())
+    for h in range(2):
+        loop(0, 8, lambda i: sib_copy(i, h).wait_recv())
     for f in range(EMB):
         w_turned[:, f * D_FIELD : (f + 1) * D_FIELD] = w_cols[f].T
 
@@ -152,6 +185,7 @@
         return send(logits.at[e], logits.at[e], lg_s.at[i], lg_r.at[i], (emb_at(i), g))
 
     loop(1, EMB, lambda i: lg_copy(i).start())
+    sent.append(lambda: loop(1, EMB, lambda i: lg_copy(i).wait_send()))
 
     for f in range(EMB):
         fields32[:, f] = fields[f].astype(F32).reshape(16, 8, SAMP)
@@ -179,21 +213,7 @@
         return send(heads.at[e], heads.at[e], hd_s.at[i], hd_r.at[i], (emb_at(i), g))
 
     loop(1, EMB, lambda i: hd_copy(i).start())
-
-    def gp_copy(i):
-        return send(pool_out.at[emb_at(i)], pool_in.at[e], gp_s.at[i], gp_r.at[i], (emb_at(i), g))
-
-    def gp_part(i):
-        f = emb_at(i)
-        pool_out[f] = jnp.dot(w_cols[f], grad, preferred_element_type=F32)
-
-    def gp_start(i):
-        gp_part(i)
-        gp_copy(i).start()
-
-    loop(1, EMB, gp_start)
-    gp_part(0)
-    pool_in[e] = pool_out[e]
+    sent.append(lambda: loop(1, EMB, lambda i: hd_copy(i).wait_send()))
 
     def grad_half(c, half):
         rhs = jnp.where(half == 0, halves[0], halves[1])
@@ -207,6 +227,41 @@
     for k, c in enumerate(order):
         y_out[c] = grad_half(c, other).astype(BF16)
         y_copy(k, c).start()
+        sent.append(lambda k=k, c=c: y_copy(k, c).wait_send())
+    core = lax.rem(e, 2)
+
+    def gs_copy(i):
+        return send(gp_sib.at[i], gp_got.at[i], gs_s.at[i], gs_r.at[i], (sib, g))
+
+    def gs_start(i):
+        gp_sib[i] = jnp.dot(w_cols[2 * i + 1 - core], grad, preferred_element_type=F32)
+        gs_copy(i).start()
+
+    loop(0, 8, gs_start)
+    sent.append(lambda: loop(0, 8, lambda i: gs_copy(i).wait_send()))
+
+    def gp_part(i):
+        gp_own[i] = jnp.dot(w_cols[2 * i + core], grad, preferred_element_type=F32)
+
+    loop(0, 8, gp_part)
+    chip = e // 2
+
+    def gp_copy(i):
+        return send(
+            gp_out.at[lax.rem(chip + i, 8)], gp_in.at[chip], gp_s.at[i], gp_r.at[i], (emb_at(2 * i), g)
+        )
+
+    def gp_start(i):
+        c = lax.rem(chip + i, 8)
+        gs_copy(c).wait_recv()
+        coded, power = encode(gp_own[c] + gp_got[c])
+        gp_out[c, :D_FIELD] = coded
+        gp_out[c, D_FIELD:] = tile_of(power)
+        gp_copy(i).start()
+
+    loop(1, 8, gp_start)
+    sent.append(lambda: loop(1, 8, lambda i: gp_copy(i).wait_send()))
+    gs_copy(chip).wait_recv()
     for k, c in enumerate(order):
         mine[c] = grad_half(c, y)
 
@@ -216,15 +271,19 @@
     for k in range(3):
         c = order[k]
         y_copy(k, c).wait_recv()
-        near_out[k] = mine[c] + y_in[c].astype(F32)
+        coded, power = encode(mine[c] + y_in[c].astype(F32))
+        near_out[k, :512] = coded
+        near_out[k, 512:] = tile_of(power)
         near_copy(k).start()
+        sent.append(lambda k=k: near_copy(k).wait_send())
     y_copy(3, zr).wait_recv()
     acc[...] = (mine[zr] + y_in[zr].astype(F32)).reshape(4, 128, 128)
 
-    loop(1, EMB, lambda i: gp_copy(i).wait_recv())
-    total = pool_in[0]
-    for f in range(1, EMB):
-        total = total + pool_in[f]
+    loop(1, 8, lambda i: gp_copy(i).wait_recv())
+    total = gp_own[chip] + gp_got[chip]
+    for i in range(1, 8):
+        c = lax.rem(chip + 8 - i, 8)
+        total = total + decode(gp_in[c, :D_FIELD], gp_in[c, D_FIELD:])
     grad_pool = total.astype(BF16)
     parts = []
     for m in range(SUB):
@@ -245,17 +304,21 @@
             )
     ty_copy = send(tab.at[other], tab_y, ty_s, ty_r, y_mate)
     ty_copy.start()
+    sent.append(lambda: ty_copy.wait_send())
 
     for k in range(3):
         near_copy(k).wait_recv()
-        acc[...] = acc[...] + near_in[k].reshape(4, 128, 128)
+        acc[...] = acc[...] + decode(near_in[k, :512], near_in[k, 512:]).reshape(4, 128, 128)
 
     def far_copy(m):
         return send(far_out.at[m - 1], far_in.at[m - 1], fr_s.at[m - 1], fr_r.at[m - 1], z_at(4 * m))
 
     for m in range(1, 4):
-        far_out[m - 1] = acc[lax.rem(zq + m, 4)]
+        coded, power = encode(acc[lax.rem(zq + m, 4)])
+        far_out[m - 1, :128] = coded
+        far_out[m - 1, 128:] = tile_of(power)
         far_copy(m).start()
+        sent.append(lambda m=m: far_copy(m).wait_send())
 
     ty_copy.wait_recv()
     tab[y] = tab[y] + tab_y[...]
@@ -265,17 +328,19 @@
 
     for k in range(3):
         tn_copy(k).start()
+        sent.append(lambda k=k: tn_copy(k).wait_send())
 
     whole = acc[zq]
     for m in range(1, 4):
         far_copy(m).wait_recv()
-        whole = whole + far_in[m - 1]
+        whole = whole + decode(far_in[m - 1, :128], far_in[m - 1, 128:])
     red[...] = whole.reshape(EMB, 8, 128)
 
     def a_copy(i):
         return send(red.at[emb_at(i)], cols.at[e], a_s.at[i], a_r.at[i], (emb_at(i), g))
 
     loop(1, EMB, lambda i: a_copy(i).start())
+    sent.append(lambda: loop(1, EMB, lambda i: a_copy(i).wait_send()))
     cols[e] = red[e]
 
     for k in range(3):
@@ -290,12 +355,19 @@
 
     for m in range(1, 4):
         tf_copy(m).start()
+        sent.append(lambda m=m: tf_copy(m).wait_send())
     for m in range(1, 4):
         tf_copy(m).wait_recv()
     tab_whole = tab[y, zr, zq] + tab_far[0] + tab_far[1] + tab_far[2]
-    out[y, zr, zq, 128:] = tab_whole
+    tab_code, tab_power = encode(tab_whole[:8])
+    head_code, head_power = encode(tab_whole[8:])
     loop(1, EMB, lambda i: a_copy(i).wait_recv())
-    out[y, zr, zq, :128] = cols[...].reshape(128, 128)
+    coded, power = encode(cols[...].reshape(128, 128))
+    spots = lax.broadcasted_iota(jnp.int32, (16, 128), 0)
+    powers = jnp.where(spots < 8, power, jnp.where(spots < 12, tab_power, head_power))
+    out[y, zr, zq, :128] = coded
+    out[y, zr, zq, 128:144] = jnp.concatenate([tab_code.astype(jnp.int32), head_code.astype(jnp.int32)], axis=0).astype(I16)
+    out[y, zr, zq, 144:] = powers.astype(jnp.int32).astype(I16)
 
     def block(off, m):
         src = lax.rem(z + 2 * ZED - off - 4 * m, ZED)
@@ -327,52 +399,42 @@
 
     for m in range(1, 4):
         of_copy(m).start()
+        sent.append(lambda m=m: of_copy(m).wait_send())
     for m in range(4):
         if m:
             of_wait(m)
         for k in range(3):
             on_copy(k, m).start()
+            sent.append(lambda k=k, m=m: on_copy(k, m).wait_send())
         oy_copy(0, m).start()
+        sent.append(lambda m=m: oy_copy(0, m).wait_send())
     for m in range(4):
         for k in range(3):
             on_wait(k, m)
             oy_copy(k + 1, m).start()
+            sent.append(lambda k=k, m=m: oy_copy(k + 1, m).wait_send())
     for m in range(4):
         for k in range(4):
             oy_wait(k, m)
-
-    loop(1, 8, lambda i: f_copy(i).wait_send())
-    loop(0, 8, lambda i: sib_copy(i).wait_send())
-
-    def sent(i):
-        w_copy(i).wait_send()
-        lg_copy(i).wait_send()
-        hd_copy(i).wait_send()
-        gp_copy(i).wait_send()
-        a_copy(i).wait_send()
-
-    loop(1, EMB, sent)
-    for k, c in enumerate(order):
-        y_copy(k, c).wait_send()
-    ty_copy.wait_send()
-    for k in range(3):
-        near_copy(k).wait_send()
-        tn_copy(k).wait_send()
-    for m in range(1, 4):
-        far_copy(m).wait_send()
-        tf_copy(m).wait_send()
-        of_copy(m).wait_send()
-    for m in range(4):
-        for k in range(3):
-            on_copy(k, m).wait_send()
-        for k in range(4):
-            oy_copy(k, m).wait_send()
-
-
-def train(pooled, low, high, w_in, w_out, labels):
-    vmem = pl.BlockSpec(memory_space=pltpu.VMEM)
+    for wait in sent:
+        wait()
+
+
+def train(codes, bag, book, w_in, w_out, labels):
+    hbm = pl.BlockSpec(memory_space=pl.ANY)
     V, D = pltpu.VMEM, pltpu.SemaphoreType.DMA
+    rows = codes.shape[1]
     scratch = [
+        V((SUB, rows), jnp.int32),
+        V((1, rows), jnp.int32),
+        V((CENT, D_FIELD), BF16),
+        V((32, 128), F32),
+        V((1, SAMP), F32),
+        V((D_FIELD, CENT), F32),
+        V((SAMP, rows), F8),
+        V((D_FIELD, SAMP), F32),
+        V((SUB * CENT, SAMP), BF16),
+        V((SUB * CENT, SAMP), BF16),
         V((EMB, D_FIELD, WIDE), BF16),
         V((WIDE, EMB * D_FIELD), BF16),
         V((EMB, D_FIELD, SAMP), BF16),
@@ -380,51 +442,56 @@
         V((4, 512, SAMP), BF16),
         V((EMB, 8, SAMP), F32),
         V((EMB, 8, 128), F32),
-        V((EMB, D_FIELD, SAMP), F32),
-        V((EMB, D_FIELD, SAMP), F32),
+        V((8, D_FIELD, SAMP), F32),
+        V((8, D_FIELD, SAMP), F32),
+        V((8, D_FIELD, SAMP), F32),
+        V((8, D_FIELD + 16, SAMP), I16),
+        V((8, D_FIELD + 16, SAMP), I16),
         V((4, 512, 128), BF16),
         V((4, 512, 128), BF16),
         V((4, 512, 128), F32),
-        V((3, 512, 128), F32),
-        V((3, 512, 128), F32),
+        V((3, 528, 128), I16),
+        V((3, 528, 128), I16),
         V((4, 128, 128), F32),
-        V((3, 128, 128), F32),
-        V((3, 128, 128), F32),
+        V((3, 144, 128), I16),
+        V((3, 144, 128), I16),
         V((EMB, 8, 128), F32),
         V((EMB, 8, 128), F32),
         V((2, 4, 4, 16, 128), F32),
         V((4, 4, 16, 128), F32),
         V((3, 4, 16, 128), F32),
         V((3, 16, 128), F32),
-        D((1,)),
+        D((6,)),
     ]
-    sems = [(16,), (8,), (8,), (16,), (16,), (16,), (4,), (3,), (3,), (16,), (), (3,), (3,), (3,), (3, 4), (4, 4)]
+    sems = [(16,), (2, 8), (2, 8), (16,), (16,), (8,), (8,), (4,), (3,), (3,), (16,), (), (3,), (3,), (3,), (3, 4), (4, 4)]
     for shape in sems:
         scratch += [D(shape), D(shape)] if shape else [D, D]
     return pl.pallas_call(
         step_kernel,
-        out_shape=jax.ShapeDtypeStruct((2, 4, 4, BLOCK, 128), F32),
-        in_specs=[vmem, vmem, vmem, pl.BlockSpec(memory_space=pl.ANY), vmem, vmem],
-        out_specs=vmem,
+        out_shape=jax.ShapeDtypeStruct((2, 4, 4, BLOCK, 128), I16),
+        in_specs=[hbm] * 6,
+        out_specs=pl.BlockSpec(memory_space=pltpu.VMEM),
         scratch_shapes=scratch,
         compiler_params=pltpu.CompilerParams(
-            collective_id=1, has_side_effects=True, vmem_limit_bytes=48 << 20
+            collective_id=1, has_side_effects=True, vmem_limit_bytes=56 << 20
         ),
         name="train_step",
-    )(pooled, low, high, w_in, w_out, labels)
+    )(codes, bag, book, w_in, w_out, labels)
 
 
 def spread_kernel(gathered, weight, table, head):
     a = pl.program_id(0)
     for c in range(4):
         for yy in range(2):
+            whole = decode(gathered[yy, c, 0, :128], gathered[yy, c, 0, 144:])
             for f in range(EMB):
                 spot = f * WIDE + yy * 128
-                weight[c * 8 : c * 8 + 8, spot : spot + 128] = gathered[yy, c, 0, f * 8 : f * 8 + 8]
-            tab = gathered[yy, c, 0, 128:]
+                weight[c * 8 : c * 8 + 8, spot : spot + 128] = whole[f * 8 : f * 8 + 8]
+            powers = number(gathered[yy, c, 0, 144:])
+            tab = number(gathered[yy, c, 0, 128:144])
             gg = yy * ZED + a * 4 + c
-            table[pl.ds(pl.multiple_of(gg * 8, 8), 8), :] = tab[:8]
-            head[pl.ds(gg, 1), :] = tab[8:9]
+            table[pl.ds(pl.multiple_of(gg * 8, 8), 8), :] = tab[:8] * jnp.exp2(powers[8:9] - 15.0)
+            head[pl.ds(gg, 1), :] = tab[8:9] * jnp.exp2(powers[12:13] - 15.0)
 
 
 def spread(gathered):
@@ -447,8 +514,9 @@
 
 
 def body(codes, row_bag, codebook, w_in, w_out, labels):
-    pooled, low, high = pool(codes[0].T, row_bag, codebook[0].T.astype(F32))
-    gathered = train(pooled, low, high, w_in, w_out.reshape(32, 128), labels.reshape(1, SAMP))
+    gathered = train(
+        codes[0].T, row_bag, codebook[0], w_in, w_out.reshape(32, 128), labels.reshape(1, SAMP)
+    )
     weight, table, head = spread(gathered)
     return table[None], weight, head.reshape(HID)
 

time: 181 us -> 119 us (0.66)
  Pallas kernels: 175 us -> 118 us
  local copies, waits for them, and re-layouts: 5.2 us -> 0 us
    pallas_call x1, Pallas kernels: 157 us -> 114 us  [train(): pl.pallas_call(step_kernel, out_shape=jax.ShapeDtypeStruct((2, 4, 4, BLOC...]
    pallas_call x1 -> x0, Pallas kernels: 13.1 us -> none  [pool(): pl.pallas_call(pool_kernel, out_shape=(jax.ShapeDtypeStruct((D_FIELD, SAM...]
    unnamed x11 -> x0, local copies, waits for them, and re-layouts: 5.2 us -> none
where the time goes in v2:
time: 119 us
  Pallas kernels  118 us (99%)
    pallas_call x1, Pallas kernels, train(): pl.pallas_call(step_kernel, out_shape=jax.ShapeDtypeStruct((2, 4, 4, BLOC...  114 us
    pallas_call x1, Pallas kernels, spread(): pl.pallas_call(spread_kernel, grid=(4,), out_shape=(jax.ShapeDtypeStruct(...  3.75 us

profile of v2, /device:TPU:6, one launch (start us, length us, event | category | flops | bytes accessed | tf_op | source)
XLA Modules:
  0.0 118.6 jit_solution(10006675168643094041)
XLA Ops:
  0.6 114.2 %train_step.1.gathered = s16[2,4,4,160,128]{4,3,2,1,0:T(8,128)(2,1)} custom-call(s32[16,3072]{1,0:T(8,128)} %bitcast.8, s32[1,3072]{1,0:T(1,128)} %bag_hbm.1, bf16[256,128]{1,0:T(8,128)(2,1)} %bitcast.9, bf16[128,4096]{1,0:T(8,128)(2,1)} %w_in.1, f32[32,128]{1,0:T(8,128)} %bitcast.10, f32[1,256]{1,0:T(1,128)} %bitcast.11), custom_call_target="tpu_custom_call" | custom-call | tf_op jit(solution)/shard_map/train_step/pallas_call | solution.py:469
  114.9 3.8 %spread.1 = (f32[128,4096]{1,0:T(8,128)}, f32[256,128]{1,0:T(8,128)}, f32[32,128]{1,0:T(8,128)}) custom-call(s16[2,4,4,160,128]{4,3,2,1,0:T(8,128)(2,1)} %train_step.1.gathered), custom_call_target="tpu_custom_call" | custom-call | tf_op jit(solution)/shard_map/spread/pallas_call | solution.py:498

commit v3 on v2

--- a/solution.py
+++ b/solution.py
@@ -23,7 +23,7 @@
 I16 = jnp.int16
 NT = (((1,), (1,)), ((), ()))
 MESH = pl.DeviceIdType.MESH
-BLOCK = 160
+BLOCK = 144
 GROUP = 4
 
 
@@ -52,8 +52,8 @@
     w_cols, w_turned, fields, fields32, turned, logits, heads,
     gp_own, gp_sib, gp_got, gp_out, gp_in,
     y_out, y_in, mine, near_out, near_in, acc, far_out, far_in, red, cols,
-    tab, tab_y, tab_near, tab_far,
-    local, w_s, w_r, f_s, f_r, sib_s, sib_r, lg_s, lg_r, hd_s, hd_r, gs_s, gs_r, gp_s, gp_r,
+    table, tab, tab_y, tab_near, tab_far,
+    local, w_s, w_r, wu_s, wu_r, wd_s, wd_r, f_s, f_r, sib_s, sib_r, lg_s, lg_r, hd_s, hd_r, gs_s, gs_r, gp_s, gp_r,
     y_s, y_r, n_s, n_r, fr_s, fr_r, a_s, a_r,
     ty_s, ty_r, tn_s, tn_r, tf_s, tf_r, of_s, of_r, on_s, on_r, oy_s, oy_r,
 ):
@@ -102,11 +102,27 @@
     for off in (1, -1, 2, -2, 4, -4, 8):
         pl.semaphore_signal(barrier, inc=1, device_id=z_at(off), device_id_type=MESH)
     pl.semaphore_signal(barrier, inc=1, device_id=y_mate, device_id_type=MESH)
-    pl.semaphore_wait(barrier, EMB - 1 + 8)
+
+    half = lax.rem(z, 2)
+    own_lanes = pl.ds(pl.multiple_of(half * 128, 128), 128)
+    far_lanes = pl.ds(pl.multiple_of((1 - half) * 128, 128), 128)
 
     def w_copy(i):
-        cols_of = pl.ds(pl.multiple_of(emb_at(i) * WIDE, WIDE), WIDE)
-        return send(w_in.at[:, cols_of], w_cols.at[e], w_s.at[i], w_r.at[i], (emb_at(i), g))
+        cols_of = pl.ds(pl.multiple_of(emb_at(i) * WIDE + half * 128, 128), 128)
+        return send(w_in.at[:, cols_of], w_cols.at[e, :, own_lanes], w_s.at[i], w_r.at[i], (emb_at(i), g))
+
+    def up_copy(i, lanes):
+        part = w_cols.at[emb_from(i), pl.ds(0, 64), lanes]
+        return send(part, part, wu_s.at[i], wu_r.at[i], z_at(1))
+
+    def down_copy(i, lanes):
+        part = w_cols.at[emb_from(i), pl.ds(64, 64), lanes]
+        return send(part, part, wd_s.at[i], wd_r.at[i], z_at(-1))
+
+    def pass_on(i):
+        w_copy(i).wait_recv()
+        up_copy(i, own_lanes).start()
+        down_copy(i, own_lanes).start()
 
     def rows_of(f, h):
         return fields.at[f, pl.ds(h * 64, 64)]
@@ -117,13 +133,6 @@
     def sib_copy(i, h):
         f = lax.rem(e + 2 * EMB - 2 * i, EMB)
         return send(rows_of(f, h), rows_of(f, h), sib_s.at[h, i], sib_r.at[h, i], (sib, g))
-
-    loop(1, EMB, lambda i: w_copy(i).start())
-    sent.append(lambda: loop(1, EMB, lambda i: w_copy(i).wait_send()))
-    own_w = pltpu.make_async_copy(
-        w_in.at[:, pl.ds(pl.multiple_of(e * WIDE, WIDE), WIDE)], w_cols.at[e], local.at[0]
-    )
-    own_w.start()
 
     def onehot(row):
         ids = lax.broadcasted_iota(jnp.int32, (CENT, row.shape[1]), 0)
@@ -153,13 +162,35 @@
                 part[mine_at], lower[span], preferred_element_type=F32
             ) + 256.0 * jnp.dot(part[mine_at], upper[span], preferred_element_type=F32)
 
-    for h in range(2):
-        loop(h * 2, h * 2 + 2, count_step)
-        fields[e, h * 64 : h * 64 + 64] = pooled[h * 64 : h * 64 + 64].astype(BF16)
+    def send_half(h):
+        rows = pl.ds(h * 64, 64)
+        fields[e, rows] = pooled[rows].astype(BF16)
         loop(1, 8, lambda i: f_copy(i, h).start())
         sib_copy(0, h).start()
-        sent.append(lambda h=h: loop(1, 8, lambda i: f_copy(i, h).wait_send()))
-        sent.append(lambda h=h: loop(0, 8, lambda i: sib_copy(i, h).wait_send()))
+        sent.append(lambda: loop(1, 8, lambda i: f_copy(i, h).wait_send()))
+        sent.append(lambda: loop(0, 8, lambda i: sib_copy(i, h).wait_send()))
+
+    loop(0, 1, count_step)
+    pl.semaphore_wait(barrier, EMB - 1 + 8)
+    loop(1, EMB, lambda i: w_copy(i).start())
+    sent.append(lambda: loop(1, EMB, lambda i: w_copy(i).wait_send()))
+    own_w = pltpu.make_async_copy(
+        w_in.at[:, pl.ds(pl.multiple_of(e * WIDE, WIDE), WIDE)], w_cols.at[e], local.at[0]
+    )
+    own_w.start()
+
+    def later_step(step):
+        count_step(step)
+
+        @pl.when(step == 1)
+        def _():
+            send_half(0)
+
+    loop(1, 4, later_step)
+    send_half(1)
+    loop(1, EMB, pass_on)
+    sent.append(lambda: loop(1, EMB, lambda i: up_copy(i, own_lanes).wait_send()))
+    sent.append(lambda: loop(1, EMB, lambda i: down_copy(i, own_lanes).wait_send()))
 
     def forward(i, h):
         f_copy(i, h).wait_recv()
@@ -167,13 +198,20 @@
 
     for h in range(2):
         loop(1, 8, lambda i: forward(i, h))
+
+    def turn(f):
+        w_turned[:, pl.ds(pl.multiple_of(f * D_FIELD, D_FIELD), D_FIELD)] = w_cols[f].T
+
+    def take(i):
+        up_copy(i, far_lanes).wait_recv()
+        down_copy(i, far_lanes).wait_recv()
+        turn(emb_from(i))
+
     own_w.wait()
-    loop(1, EMB, lambda i: w_copy(i).wait_recv())
+    turn(e)
+    loop(1, EMB, take)
     for h in range(2):
         loop(0, 8, lambda i: sib_copy(i, h).wait_recv())
-    for f in range(EMB):
-        w_turned[:, f * D_FIELD : (f + 1) * D_FIELD] = w_cols[f].T
-
     pre = jnp.dot(w_turned[...], fields[...].reshape(EMB * D_FIELD, SAMP), preferred_element_type=F32)
     gate = jax.nn.sigmoid(pre)
     act = pre * gate
@@ -225,7 +263,9 @@
     near = (2, 1, -1)
     order = [lax.rem(z + off + 4, 4) for off in near] + [zr]
     for k, c in enumerate(order):
-        y_out[c] = grad_half(c, other).astype(BF16)
+        coded, power = encode(grad_half(c, other))
+        y_out[c, :512] = coded
+        y_out[c, 512:] = tile_of(power)
         y_copy(k, c).start()
         sent.append(lambda k=k, c=c: y_copy(k, c).wait_send())
     core = lax.rem(e, 2)
@@ -271,13 +311,13 @@
     for k in range(3):
         c = order[k]
         y_copy(k, c).wait_recv()
-        coded, power = encode(mine[c] + y_in[c].astype(F32))
+        coded, power = encode(mine[c] + decode(y_in[c, :512], y_in[c, 512:]))
         near_out[k, :512] = coded
         near_out[k, 512:] = tile_of(power)
         near_copy(k).start()
         sent.append(lambda k=k: near_copy(k).wait_send())
     y_copy(3, zr).wait_recv()
-    acc[...] = (mine[zr] + y_in[zr].astype(F32)).reshape(4, 128, 128)
+    acc[...] = (mine[zr] + decode(y_in[zr, :512], y_in[zr, 512:])).reshape(4, 128, 128)
 
     loop(1, 8, lambda i: gp_copy(i).wait_recv())
     total = gp_own[chip] + gp_got[chip]
@@ -285,15 +325,18 @@
         c = lax.rem(chip + 8 - i, 8)
         total = total + decode(gp_in[c, :D_FIELD], gp_in[c, D_FIELD:])
     grad_pool = total.astype(BF16)
-    parts = []
-    for m in range(SUB):
-        rows = grad_pool[m * SUBW : (m + 1) * SUBW]
-        span = slice(m * CENT, (m + 1) * CENT)
-        parts.append(
-            lax.dot_general(rows, low[span, :], NT, preferred_element_type=F32)
-            + 256.0 * lax.dot_general(rows, high[span, :], NT, preferred_element_type=F32)
-        )
-    table = jnp.concatenate(parts, axis=0).T
+    subs = lax.broadcasted_iota(jnp.int32, (CENT, D_FIELD), 1) // SUBW
+    table[...] = jnp.zeros((CENT, D_FIELD), F32)
+
+    def table_step(step):
+        place = pl.ds(pl.multiple_of(step * GROUP * CENT, GROUP * CENT), GROUP * CENT)
+        got = lax.dot_general(low[place, :], grad_pool, NT, preferred_element_type=F32)
+        got = got + 256.0 * lax.dot_general(high[place, :], grad_pool, NT, preferred_element_type=F32)
+        for j in range(GROUP):
+            part = got[j * CENT : (j + 1) * CENT]
+            table[...] = table[...] + jnp.where(subs == step * GROUP + j, part, 0.0)
+
+    loop(0, SUB // GROUP, table_step)
     loop(1, EMB, lambda i: hd_copy(i).wait_recv())
     for yy in range(2):
         for zz in range(ZED):
@@ -364,11 +407,11 @@
     loop(1, EMB, lambda i: a_copy(i).wait_recv())
     coded, power = encode(cols[...].reshape(128, 128))
     spots = lax.broadcasted_iota(jnp.int32, (16, 128), 0)
-    powers = jnp.where(spots < 8, power, jnp.where(spots < 12, tab_power, head_power))
+    tail = jnp.concatenate([number(tab_code), number(head_code)], axis=0)
+    for at, row in ((9, power), (10, tab_power), (11, head_power)):
+        tail = jnp.where(spots == at, row, tail)
     out[y, zr, zq, :128] = coded
-    out[y, zr, zq, 128:144] = jnp.concatenate([tab_code.astype(jnp.int32), head_code.astype(jnp.int32)], axis=0).astype(I16)
-    out[y, zr, zq, 144:] = powers.astype(jnp.int32).astype(I16)
-
+    out[y, zr, zq, 128:] = tail.astype(jnp.int32).astype(I16)
     def block(off, m):
         src = lax.rem(z + 2 * ZED - off - 4 * m, ZED)
         return out.at[y, lax.rem(src, 4), src // 4]
@@ -447,8 +490,8 @@
         V((8, D_FIELD, SAMP), F32),
         V((8, D_FIELD + 16, SAMP), I16),
         V((8, D_FIELD + 16, SAMP), I16),
-        V((4, 512, 128), BF16),
-        V((4, 512, 128), BF16),
+        V((4, 528, 128), I16),
+        V((4, 528, 128), I16),
         V((4, 512, 128), F32),
         V((3, 528, 128), I16),
         V((3, 528, 128), I16),
@@ -457,13 +500,14 @@
         V((3, 144, 128), I16),
         V((EMB, 8, 128), F32),
         V((EMB, 8, 128), F32),
+        V((CENT, D_FIELD), F32),
         V((2, 4, 4, 16, 128), F32),
         V((4, 4, 16, 128), F32),
         V((3, 4, 16, 128), F32),
         V((3, 16, 128), F32),
         D((6,)),
     ]
-    sems = [(16,), (2, 8), (2, 8), (16,), (16,), (8,), (8,), (4,), (3,), (3,), (16,), (), (3,), (3,), (3,), (3, 4), (4, 4)]
+    sems = [(16,), (16,), (16,), (2, 8), (2, 8), (16,), (16,), (8,), (8,), (4,), (3,), (3,), (16,), (), (3,), (3,), (3,), (3, 4), (4, 4)]
     for shape in sems:
         scratch += [D(shape), D(shape)] if shape else [D, D]
     return pl.pallas_call(
@@ -483,15 +527,15 @@
     a = pl.program_id(0)
     for c in range(4):
         for yy in range(2):
-            whole = decode(gathered[yy, c, 0, :128], gathered[yy, c, 0, 144:])
+            tail = number(gathered[yy, c, 0, 128:])
+            scales = jnp.exp2(tail[8:] - 15.0)
+            whole = number(gathered[yy, c, 0, :128]) * scales[1:2]
             for f in range(EMB):
                 spot = f * WIDE + yy * 128
                 weight[c * 8 : c * 8 + 8, spot : spot + 128] = whole[f * 8 : f * 8 + 8]
-            powers = number(gathered[yy, c, 0, 144:])
-            tab = number(gathered[yy, c, 0, 128:144])
             gg = yy * ZED + a * 4 + c
-            table[pl.ds(pl.multiple_of(gg * 8, 8), 8), :] = tab[:8] * jnp.exp2(powers[8:9] - 15.0)
-            head[pl.ds(gg, 1), :] = tab[8:9] * jnp.exp2(powers[12:13] - 15.0)
+            table[pl.ds(pl.multiple_of(gg * 8, 8), 8), :] = tail[:8] * scales[2:3]
+            head[pl.ds(gg, 1), :] = tail[8:9] * scales[3:4]
 
 
 def spread(gathered):

time: 119 us -> 113 us (0.950)
  the two profiles are of different devices: /device:TPU:6 before, /device:TPU:72 now
where the time goes in v3:
time: 113 us
  Pallas kernels  113 us (100%)
    pallas_call x1, Pallas kernels, train(): pl.pallas_call(step_kernel, out_shape=jax.ShapeDtypeStruct((2, 4, 4, BLOC...  109 us
    pallas_call x1, Pallas kernels, spread(): pl.pallas_call(spread_kernel, grid=(4,), out_shape=(jax.ShapeDtypeStruct(...  3.72 us

profile of v3, /device:TPU:72, one launch (start us, length us, event | category | flops | bytes accessed | tf_op | source)
XLA Modules:
  0.0 113.3 jit_solution(13943947441175370425)
XLA Ops:
  0.6 108.9 %train_step.1.gathered = s16[2,4,4,144,128]{4,3,2,1,0:T(8,128)(2,1)} custom-call(s32[16,3072]{1,0:T(8,128)} %bitcast.8, s32[1,3072]{1,0:T(1,128)} %bag_hbm.1, bf16[256,128]{1,0:T(8,128)(2,1)} %bitcast.9, bf16[128,4096]{1,0:T(8,128)(2,1)} %w_in.1, f32[32,128]{1,0:T(8,128)} %bitcast.10, f32[1,256]{1,0:T(1,128)} %bitcast.11), custom_call_target="tpu_custom_call" | custom-call | tf_op jit(solution)/shard_map/train_step/pallas_call | solution.py:513
  109.6 3.7 %spread.1 = (f32[128,4096]{1,0:T(8,128)}, f32[256,128]{1,0:T(8,128)}, f32[32,128]{1,0:T(8,128)}) custom-call(s16[2,4,4,144,128]{4,3,2,1,0:T(8,128)(2,1)} %train_step.1.gathered), custom_call_target="tpu_custom_call" | custom-call | tf_op jit(solution)/shard_map/spread/pallas_call | solution.py:542

commit v4 on v3

--- a/solution.py
+++ b/solution.py
@@ -52,10 +52,10 @@
     w_cols, w_turned, fields, fields32, turned, logits, heads,
     gp_own, gp_sib, gp_got, gp_out, gp_in,
     y_out, y_in, mine, near_out, near_in, acc, far_out, far_in, red, cols,
-    table, tab, tab_y, tab_near, tab_far,
+    table, tab, tab_y, tab_near, tab_far, tabs,
     local, w_s, w_r, wu_s, wu_r, wd_s, wd_r, f_s, f_r, sib_s, sib_r, lg_s, lg_r, hd_s, hd_r, gs_s, gs_r, gp_s, gp_r,
     y_s, y_r, n_s, n_r, fr_s, fr_r, a_s, a_r,
-    ty_s, ty_r, tn_s, tn_r, tf_s, tf_r, of_s, of_r, on_s, on_r, oy_s, oy_r,
+    ty_s, ty_r, tn_s, tn_r, tf_s, tf_r, tg_s, tg_r, on_s, on_r, oy_s, oy_r,
 ):
     e = lax.axis_index("emb")
     g = lax.axis_index("dense")
@@ -135,8 +135,9 @@
         return send(rows_of(f, h), rows_of(f, h), sib_s.at[h, i], sib_r.at[h, i], (sib, g))
 
     def onehot(row):
-        ids = lax.broadcasted_iota(jnp.int32, (CENT, row.shape[1]), 0)
-        return jnp.where(row == ids, 1.0, 0.0).astype(F8)
+        ids = lax.broadcasted_iota(jnp.int32, (CENT, row.shape[1]), 0).astype(F32).astype(BF16)
+        same = row.astype(F32).astype(BF16) == ids
+        return jnp.where(same, jnp.ones((), BF16), jnp.zeros((), BF16)).astype(F8)
 
     for load in loads:
         load.wait()
@@ -244,15 +245,6 @@
     grad = (slope[:1] * w_tall * slant).astype(BF16)
     halves = (grad[:128], grad[128:])
 
-    head = lax.dot_general(slope, act, NT, precision=lax.Precision.HIGHEST, preferred_element_type=F32)
-    heads[e] = jnp.concatenate([head[:1, :128], head[:1, 128:], jnp.zeros((6, 128), F32)], axis=0)
-
-    def hd_copy(i):
-        return send(heads.at[e], heads.at[e], hd_s.at[i], hd_r.at[i], (emb_at(i), g))
-
-    loop(1, EMB, lambda i: hd_copy(i).start())
-    sent.append(lambda: loop(1, EMB, lambda i: hd_copy(i).wait_send()))
-
     def grad_half(c, half):
         rhs = jnp.where(half == 0, halves[0], halves[1])
         return lax.dot_general(turned[c], rhs, NT, preferred_element_type=F32)
@@ -268,6 +260,15 @@
         y_out[c, 512:] = tile_of(power)
         y_copy(k, c).start()
         sent.append(lambda k=k, c=c: y_copy(k, c).wait_send())
+    head = lax.dot_general(slope, act, NT, precision=lax.Precision.HIGHEST, preferred_element_type=F32)
+    heads[e] = jnp.concatenate([head[:1, :128], head[:1, 128:], jnp.zeros((6, 128), F32)], axis=0)
+
+    def hd_copy(i):
+        return send(heads.at[e], heads.at[e], hd_s.at[i], hd_r.at[i], (emb_at(i), g))
+
+    loop(1, EMB, lambda i: hd_copy(i).start())
+    sent.append(lambda: loop(1, EMB, lambda i: hd_copy(i).wait_send()))
+
     core = lax.rem(e, 2)
 
     def gs_copy(i):
@@ -373,63 +374,71 @@
         tn_copy(k).start()
         sent.append(lambda k=k: tn_copy(k).wait_send())
 
+    for k in range(3):
+        tn_copy(k).wait_recv()
+    tab_sum = tab[y, zr] + tab_near[0] + tab_near[1] + tab_near[2]
+    tab[y, zr] = tab_sum
+
+    def tf_copy(m):
+        return send(
+            tab.at[y, zr, lax.rem(zq + m, 4)], tab_far.at[m - 1], tf_s.at[m - 1], tf_r.at[m - 1], z_at(4 * m)
+        )
+
+    for m in range(1, 4):
+        tf_copy(m).start()
+        sent.append(lambda m=m: tf_copy(m).wait_send())
     whole = acc[zq]
     for m in range(1, 4):
         far_copy(m).wait_recv()
         whole = whole + decode(far_in[m - 1, :128], far_in[m - 1, 128:])
     red[...] = whole.reshape(EMB, 8, 128)
 
-    def a_copy(i):
-        return send(red.at[emb_at(i)], cols.at[e], a_s.at[i], a_r.at[i], (emb_at(i), g))
-
-    loop(1, EMB, lambda i: a_copy(i).start())
-    sent.append(lambda: loop(1, EMB, lambda i: a_copy(i).wait_send()))
-    cols[e] = red[e]
-
-    for k in range(3):
-        tn_copy(k).wait_recv()
-    tab_sum = tab[y, zr] + tab_near[0] + tab_near[1] + tab_near[2]
-    tab[y, zr] = tab_sum
-
-    def tf_copy(m):
-        return send(
-            tab.at[y, zr, lax.rem(zq + m, 4)], tab_far.at[m - 1], tf_s.at[m - 1], tf_r.at[m - 1], z_at(4 * m)
-        )
-
-    for m in range(1, 4):
-        tf_copy(m).start()
-        sent.append(lambda m=m: tf_copy(m).wait_send())
+    def a_copy(m, i):
+        to = (emb_at(i), y * ZED + lax.rem(z + 4 * m, ZED))
+        return send(red.at[emb_at(i)], cols.at[m, e], a_s.at[m, i], a_r.at[m, i], to)
+
+    for m in (2, 1, 3, 0):
+        first = 1 if m == 0 else 0
+        loop(first, EMB, lambda i: a_copy(m, i).start())
+        sent.append(lambda m=m, first=first: loop(first, EMB, lambda i: a_copy(m, i).wait_send()))
+    cols[0, e] = red[e]
+
     for m in range(1, 4):
         tf_copy(m).wait_recv()
-    tab_whole = tab[y, zr, zq] + tab_far[0] + tab_far[1] + tab_far[2]
-    tab_code, tab_power = encode(tab_whole[:8])
-    head_code, head_power = encode(tab_whole[8:])
-    loop(1, EMB, lambda i: a_copy(i).wait_recv())
-    coded, power = encode(cols[...].reshape(128, 128))
-    spots = lax.broadcasted_iota(jnp.int32, (16, 128), 0)
-    tail = jnp.concatenate([number(tab_code), number(head_code)], axis=0)
-    for at, row in ((9, power), (10, tab_power), (11, head_power)):
-        tail = jnp.where(spots == at, row, tail)
-    out[y, zr, zq, :128] = coded
-    out[y, zr, zq, 128:] = tail.astype(jnp.int32).astype(I16)
+    tabs[0] = tab[y, zr, zq] + tab_far[0] + tab_far[1] + tab_far[2]
+
+    def tg_copy(m):
+        return send(tabs.at[0], tabs.at[m], tg_s.at[m - 1], tg_r.at[m - 1], z_at(4 * m))
+
+    for m in range(1, 4):
+        tg_copy(m).start()
+        sent.append(lambda m=m: tg_copy(m).wait_send())
+
     def block(off, m):
         src = lax.rem(z + 2 * ZED - off - 4 * m, ZED)
         return out.at[y, lax.rem(src, 4), src // 4]
 
-    def of_copy(m):
-        return send(block(0, 0), block(0, 0), of_s.at[m - 1], of_r.at[m - 1], z_at(4 * m))
-
-    def of_wait(m):
-        send(block(0, m), block(0, m), of_s.at[m - 1], of_r.at[m - 1], z_at(4 * m)).wait_recv()
+    def pack(m):
+        tab_code, tab_power = encode(tabs[m, :8])
+        head_code, head_power = encode(tabs[m, 8:])
+        coded, power = encode(cols[m].reshape(128, 128))
+        spots = lax.broadcasted_iota(jnp.int32, (16, 128), 0)
+        tail = jnp.concatenate([number(tab_code), number(head_code)], axis=0)
+        for at, row in ((9, power), (10, tab_power), (11, head_power)):
+            tail = jnp.where(spots == at, row, tail)
+        here = block(0, m)
+        here[:128] = coded
+        here[128:] = tail.astype(jnp.int32).astype(I16)
 
     ways = (1, -1, 2)
 
     def on_copy(k, m):
-        return send(block(0, m), block(0, m), on_s.at[k, m], on_r.at[k, m], z_at(ways[k]))
+        got = block(1 if k == 2 else 0, m)
+        return send(got, got, on_s.at[k, m], on_r.at[k, m], z_at(-1 if k == 1 else 1))
 
     def on_wait(k, m):
         got = block(ways[k], m)
-        send(got, got, on_s.at[k, m], on_r.at[k, m], z_at(ways[k])).wait_recv()
+        send(got, got, on_s.at[k, m], on_r.at[k, m], z_at(1)).wait_recv()
 
     def oy_copy(k, m):
         got = block(0 if k == 0 else ways[k - 1], m)
@@ -440,22 +449,28 @@
         got = out.at[other, lax.rem(src, 4), src // 4]
         send(got, got, oy_s.at[k, m], oy_r.at[k, m], y_mate).wait_recv()
 
-    for m in range(1, 4):
-        of_copy(m).start()
-        sent.append(lambda m=m: of_copy(m).wait_send())
-    for m in range(4):
+    def put(copy):
+        copy.start()
+        sent.append(copy.wait_send)
+
+    turns = (0, 1, 3, 2)
+    for m in turns:
+        loop(1 if m == 0 else 0, EMB, lambda i: a_copy(m, i).wait_recv())
         if m:
-            of_wait(m)
-        for k in range(3):
-            on_copy(k, m).start()
-            sent.append(lambda k=k, m=m: on_copy(k, m).wait_send())
-        oy_copy(0, m).start()
-        sent.append(lambda m=m: oy_copy(0, m).wait_send())
-    for m in range(4):
-        for k in range(3):
-            on_wait(k, m)
-            oy_copy(k + 1, m).start()
-            sent.append(lambda k=k, m=m: oy_copy(k + 1, m).wait_send())
+            tg_copy(m).wait_recv()
+        pack(m)
+        put(on_copy(0, m))
+        put(on_copy(1, m))
+        put(oy_copy(0, m))
+    for m in turns:
+        on_wait(0, m)
+        put(on_copy(2, m))
+        put(oy_copy(1, m))
+        on_wait(1, m)
+        put(oy_copy(2, m))
+    for m in turns:
+        on_wait(2, m)
+        put(oy_copy(3, m))
     for m in range(4):
         for k in range(4):
             oy_wait(k, m)
@@ -499,15 +514,16 @@
         V((3, 144, 128), I16),
         V((3, 144, 128), I16),
         V((EMB, 8, 128), F32),
-        V((EMB, 8, 128), F32),
+        V((4, EMB, 8, 128), F32),
         V((CENT, D_FIELD), F32),
         V((2, 4, 4, 16, 128), F32),
         V((4, 4, 16, 128), F32),
         V((3, 4, 16, 128), F32),
         V((3, 16, 128), F32),
+        V((4, 16, 128), F32),
         D((6,)),
     ]
-    sems = [(16,), (16,), (16,), (2, 8), (2, 8), (16,), (16,), (8,), (8,), (4,), (3,), (3,), (16,), (), (3,), (3,), (3,), (3, 4), (4, 4)]
+    sems = [(16,), (16,), (16,), (2, 8), (2, 8), (16,), (16,), (8,), (8,), (4,), (3,), (3,), (4, 16), (), (3,), (3,), (3,), (3, 4), (4, 4)]
     for shape in sems:
         scratch += [D(shape), D(shape)] if shape else [D, D]
     return pl.pallas_call(

time: 113 us -> 115 us (1.018)
  the two profiles are of different devices: /device:TPU:72 before, /device:TPU:6 now
where the time goes in v4:
time: 115 us; the launch traced here: 114 us
  Pallas kernels  113 us (98%)
    pallas_call x1, Pallas kernels, train(): pl.pallas_call(step_kernel, out_shape=jax.ShapeDtypeStruct((2, 4, 4, BLOC...  109 us
    pallas_call x1, Pallas kernels, spread(): pl.pallas_call(spread_kernel, grid=(4,), out_shape=(jax.ShapeDtypeStruct(...  3.72 us

profile of v4, /device:TPU:6, one launch (start us, length us, event | category | flops | bytes accessed | tf_op | source)
XLA Modules:
  0.0 113.7 jit_solution(4611395159207810307)
XLA Ops:
  0.6 109.3 %train_step.1.gathered = s16[2,4,4,144,128]{4,3,2,1,0:T(8,128)(2,1)} custom-call(s32[16,3072]{1,0:T(8,128)} %bitcast.8, s32[1,3072]{1,0:T(1,128)} %bag_hbm.1, bf16[256,128]{1,0:T(8,128)(2,1)} %bitcast.9, bf16[128,4096]{1,0:T(8,128)(2,1)} %w_in.1, f32[32,128]{1,0:T(8,128)} %bitcast.10, f32[1,256]{1,0:T(1,128)} %bitcast.11), custom_call_target="tpu_custom_call" | custom-call | tf_op jit(solution)/shard_map/train_step/pallas_call | solution.py:529
  110.0 3.7 %spread.1 = (f32[128,4096]{1,0:T(8,128)}, f32[256,128]{1,0:T(8,128)}, f32[32,128]{1,0:T(8,128)}) custom-call(s16[2,4,4,144,128]{4,3,2,1,0:T(8,128)(2,1)} %train_step.1.gathered), custom_call_target="tpu_custom_call" | custom-call | tf_op jit(solution)/shard_map/spread/pallas_call | solution.py:558

commit v5 on v4

--- a/solution.py
+++ b/solution.py
@@ -50,12 +50,12 @@
     codes_hbm, bag_hbm, book_hbm, w_in, w_out_hbm, labels_hbm, out,
     codes, bag, book, w_out, labels, table_t, members, pooled, low, high,
     w_cols, w_turned, fields, fields32, turned, logits, heads,
-    gp_own, gp_sib, gp_got, gp_out, gp_in,
+    gp_own, gp_sib, gp_got, gp_out, gp_in, gq_out, gq_in, gp_sum,
     y_out, y_in, mine, near_out, near_in, acc, far_out, far_in, red, cols,
-    table, tab, tab_y, tab_near, tab_far, tabs,
-    local, w_s, w_r, wu_s, wu_r, wd_s, wd_r, f_s, f_r, sib_s, sib_r, lg_s, lg_r, hd_s, hd_r, gs_s, gs_r, gp_s, gp_r,
+    table, tab, tab_y, tab_near, tab_far,
+    local, w_s, w_r, wu_s, wu_r, wd_s, wd_r, f_s, f_r, sib_s, sib_r, lg_s, lg_r, hd_s, hd_r, gs_s, gs_r, gp_s, gp_r, gq_s, gq_r,
     y_s, y_r, n_s, n_r, fr_s, fr_r, a_s, a_r,
-    ty_s, ty_r, tn_s, tn_r, tf_s, tf_r, tg_s, tg_r, on_s, on_r, oy_s, oy_r,
+    ty_s, ty_r, tn_s, tn_r, tf_s, tf_r, of_s, of_r, on_s, on_r, oy_s, oy_r,
 ):
     e = lax.axis_index("emb")
     g = lax.axis_index("dense")
@@ -286,23 +286,26 @@
 
     loop(0, 8, gp_part)
     chip = e // 2
+    y_high = chip // 4
+    col = lax.rem(chip, 4)
 
     def gp_copy(i):
-        return send(
-            gp_out.at[lax.rem(chip + i, 8)], gp_in.at[chip], gp_s.at[i], gp_r.at[i], (emb_at(2 * i), g)
-        )
+        to = (y_high * 8 + 2 * lax.rem(col + i, 4) + core, g)
+        return send(gp_out.at[i - 1], gp_in.at[i - 1], gp_s.at[i - 1], gp_r.at[i - 1], to)
 
     def gp_start(i):
-        c = lax.rem(chip + i, 8)
-        gs_copy(c).wait_recv()
-        coded, power = encode(gp_own[c] + gp_got[c])
-        gp_out[c, :D_FIELD] = coded
-        gp_out[c, D_FIELD:] = tile_of(power)
+        for h in range(2):
+            c = h * 4 + lax.rem(col + i, 4)
+            gs_copy(c).wait_recv()
+            coded, power = encode(gp_own[c] + gp_got[c])
+            gp_out[i - 1, h, :D_FIELD] = coded
+            gp_out[i - 1, h, D_FIELD:] = tile_of(power)
         gp_copy(i).start()
 
-    loop(1, 8, gp_start)
-    sent.append(lambda: loop(1, 8, lambda i: gp_copy(i).wait_send()))
-    gs_copy(chip).wait_recv()
+    loop(1, 4, gp_start)
+    sent.append(lambda: loop(1, 4, lambda i: gp_copy(i).wait_send()))
+    for h in range(2):
+        gs_copy(h * 4 + col).wait_recv()
     for k, c in enumerate(order):
         mine[c] = grad_half(c, y)
 
@@ -320,12 +323,38 @@
     y_copy(3, zr).wait_recv()
     acc[...] = (mine[zr] + decode(y_in[zr, :512], y_in[zr, 512:])).reshape(4, 128, 128)
 
-    loop(1, 8, lambda i: gp_copy(i).wait_recv())
-    total = gp_own[chip] + gp_got[chip]
-    for i in range(1, 8):
-        c = lax.rem(chip + 8 - i, 8)
-        total = total + decode(gp_in[c, :D_FIELD], gp_in[c, D_FIELD:])
-    grad_pool = total.astype(BF16)
+    loop(1, 4, lambda i: gp_copy(i).wait_recv())
+
+    def row_sum(h):
+        total = gp_own[h * 4 + col] + gp_got[h * 4 + col]
+        for i in range(3):
+            total = total + decode(gp_in[i, h, :D_FIELD], gp_in[i, h, D_FIELD:])
+        return total
+
+    coded, power = encode(row_sum(1 - y_high))
+    gq_out[:D_FIELD] = coded
+    gq_out[D_FIELD:] = tile_of(power)
+    gq_copy = send(gq_out, gq_in, gq_s, gq_r, (emb_at(8), g))
+    gq_copy.start()
+    sent.append(lambda: gq_copy.wait_send())
+    gp_sum[...] = row_sum(y_high)
+
+    for k in range(3):
+        near_copy(k).wait_recv()
+        acc[...] = acc[...] + decode(near_in[k, :512], near_in[k, 512:]).reshape(4, 128, 128)
+
+    def far_copy(m):
+        return send(far_out.at[m - 1], far_in.at[m - 1], fr_s.at[m - 1], fr_r.at[m - 1], z_at(4 * m))
+
+    for m in (2, 1, 3):
+        coded, power = encode(acc[lax.rem(zq + m, 4)])
+        far_out[m - 1, :128] = coded
+        far_out[m - 1, 128:] = tile_of(power)
+        far_copy(m).start()
+        sent.append(lambda m=m: far_copy(m).wait_send())
+
+    gq_copy.wait_recv()
+    grad_pool = (gp_sum[...] + decode(gq_in[:D_FIELD], gq_in[D_FIELD:])).astype(BF16)
     subs = lax.broadcasted_iota(jnp.int32, (CENT, D_FIELD), 1) // SUBW
     table[...] = jnp.zeros((CENT, D_FIELD), F32)
 
@@ -349,21 +378,6 @@
     ty_copy = send(tab.at[other], tab_y, ty_s, ty_r, y_mate)
     ty_copy.start()
     sent.append(lambda: ty_copy.wait_send())
-
-    for k in range(3):
-        near_copy(k).wait_recv()
-        acc[...] = acc[...] + decode(near_in[k, :512], near_in[k, 512:]).reshape(4, 128, 128)
-
-    def far_copy(m):
-        return send(far_out.at[m - 1], far_in.at[m - 1], fr_s.at[m - 1], fr_r.at[m - 1], z_at(4 * m))
-
-    for m in range(1, 4):
-        coded, power = encode(acc[lax.rem(zq + m, 4)])
-        far_out[m - 1, :128] = coded
-        far_out[m - 1, 128:] = tile_of(power)
-        far_copy(m).start()
-        sent.append(lambda m=m: far_copy(m).wait_send())
-
     ty_copy.wait_recv()
     tab[y] = tab[y] + tab_y[...]
 
@@ -373,11 +387,9 @@
     for k in range(3):
         tn_copy(k).start()
         sent.append(lambda k=k: tn_copy(k).wait_send())
-
     for k in range(3):
         tn_copy(k).wait_recv()
-    tab_sum = tab[y, zr] + tab_near[0] + tab_near[1] + tab_near[2]
-    tab[y, zr] = tab_sum
+    tab[y, zr] = tab[y, zr] + tab_near[0] + tab_near[1] + tab_near[2]
 
     def tf_copy(m):
         return send(
@@ -387,48 +399,42 @@
     for m in range(1, 4):
         tf_copy(m).start()
         sent.append(lambda m=m: tf_copy(m).wait_send())
+
     whole = acc[zq]
     for m in range(1, 4):
         far_copy(m).wait_recv()
         whole = whole + decode(far_in[m - 1, :128], far_in[m - 1, 128:])
     red[...] = whole.reshape(EMB, 8, 128)
 
-    def a_copy(m, i):
-        to = (emb_at(i), y * ZED + lax.rem(z + 4 * m, ZED))
-        return send(red.at[emb_at(i)], cols.at[m, e], a_s.at[m, i], a_r.at[m, i], to)
-
-    for m in (2, 1, 3, 0):
-        first = 1 if m == 0 else 0
-        loop(first, EMB, lambda i: a_copy(m, i).start())
-        sent.append(lambda m=m, first=first: loop(first, EMB, lambda i: a_copy(m, i).wait_send()))
-    cols[0, e] = red[e]
+    def a_copy(i):
+        return send(red.at[emb_at(i)], cols.at[e], a_s.at[i], a_r.at[i], (emb_at(i), g))
+
+    loop(1, EMB, lambda i: a_copy(i).start())
+    sent.append(lambda: loop(1, EMB, lambda i: a_copy(i).wait_send()))
+    cols[e] = red[e]
 
     for m in range(1, 4):
         tf_copy(m).wait_recv()
-    tabs[0] = tab[y, zr, zq] + tab_far[0] + tab_far[1] + tab_far[2]
-
-    def tg_copy(m):
-        return send(tabs.at[0], tabs.at[m], tg_s.at[m - 1], tg_r.at[m - 1], z_at(4 * m))
-
-    for m in range(1, 4):
-        tg_copy(m).start()
-        sent.append(lambda m=m: tg_copy(m).wait_send())
-
+    tab_whole = tab[y, zr, zq] + tab_far[0] + tab_far[1] + tab_far[2]
+    tab_code, tab_power = encode(tab_whole[:8])
+    head_code, head_power = encode(tab_whole[8:])
+    loop(1, EMB, lambda i: a_copy(i).wait_recv())
+    coded, power = encode(cols[...].reshape(128, 128))
+    spots = lax.broadcasted_iota(jnp.int32, (16, 128), 0)
+    tail = jnp.concatenate([number(tab_code), number(head_code)], axis=0)
+    for at, row in ((9, power), (10, tab_power), (11, head_power)):
+        tail = jnp.where(spots == at, row, tail)
+    out[y, zr, zq, :128] = coded
+    out[y, zr, zq, 128:] = tail.astype(jnp.int32).astype(I16)
     def block(off, m):
         src = lax.rem(z + 2 * ZED - off - 4 * m, ZED)
         return out.at[y, lax.rem(src, 4), src // 4]
 
-    def pack(m):
-        tab_code, tab_power = encode(tabs[m, :8])
-        head_code, head_power = encode(tabs[m, 8:])
-        coded, power = encode(cols[m].reshape(128, 128))
-        spots = lax.broadcasted_iota(jnp.int32, (16, 128), 0)
-        tail = jnp.concatenate([number(tab_code), number(head_code)], axis=0)
-        for at, row in ((9, power), (10, tab_power), (11, head_power)):
-            tail = jnp.where(spots == at, row, tail)
-        here = block(0, m)
-        here[:128] = coded
-        here[128:] = tail.astype(jnp.int32).astype(I16)
+    def of_copy(m):
+        return send(block(0, 0), block(0, 0), of_s.at[m - 1], of_r.at[m - 1], z_at(4 * m))
+
+    def of_wait(m):
+        send(block(0, m), block(0, m), of_s.at[m - 1], of_r.at[m - 1], z_at(4 * m)).wait_recv()
 
     ways = (1, -1, 2)
 
@@ -454,11 +460,11 @@
         sent.append(copy.wait_send)
 
     turns = (0, 1, 3, 2)
+    for m in (2, 1, 3):
+        put(of_copy(m))
     for m in turns:
-        loop(1 if m == 0 else 0, EMB, lambda i: a_copy(m, i).wait_recv())
         if m:
-            tg_copy(m).wait_recv()
-        pack(m)
+            of_wait(m)
         put(on_copy(0, m))
         put(on_copy(1, m))
         put(oy_copy(0, m))
@@ -503,8 +509,11 @@
         V((8, D_FIELD, SAMP), F32),
         V((8, D_FIELD, SAMP), F32),
         V((8, D_FIELD, SAMP), F32),
-        V((8, D_FIELD + 16, SAMP), I16),
-        V((8, D_FIELD + 16, SAMP), I16),
+        V((3, 2, D_FIELD + 16, SAMP), I16),
+        V((3, 2, D_FIELD + 16, SAMP), I16),
+        V((D_FIELD + 16, SAMP), I16),
+        V((D_FIELD + 16, SAMP), I16),
+        V((D_FIELD, SAMP), F32),
         V((4, 528, 128), I16),
         V((4, 528, 128), I16),
         V((4, 512, 128), F32),
@@ -514,16 +523,15 @@
         V((3, 144, 128), I16),
         V((3, 144, 128), I16),
         V((EMB, 8, 128), F32),
-        V((4, EMB, 8, 128), F32),
+        V((EMB, 8, 128), F32),
         V((CENT, D_FIELD), F32),
         V((2, 4, 4, 16, 128), F32),
         V((4, 4, 16, 128), F32),
         V((3, 4, 16, 128), F32),
         V((3, 16, 128), F32),
-        V((4, 16, 128), F32),
         D((6,)),
     ]
-    sems = [(16,), (16,), (16,), (2, 8), (2, 8), (16,), (16,), (8,), (8,), (4,), (3,), (3,), (4, 16), (), (3,), (3,), (3,), (3, 4), (4, 4)]
+    sems = [(16,), (16,), (16,), (2, 8), (2, 8), (16,), (16,), (8,), (3,), (), (4,), (3,), (3,), (16,), (), (3,), (3,), (3,), (3, 4), (4, 4)]
     for shape in sems:
         scratch += [D(shape), D(shape)] if shape else [D, D]
     return pl.pallas_call(

time: 115 us -> 105 us (0.913)
  the two profiles are of different devices: /device:TPU:6 before, /device:TPU:16 now
where the time goes in v5:
time: 105 us
  Pallas kernels  104 us (99%)
    pallas_call x1, Pallas kernels, train(): pl.pallas_call(step_kernel, out_shape=jax.ShapeDtypeStruct((2, 4, 4, BLOC...  100 us
    pallas_call x1, Pallas kernels, spread(): pl.pallas_call(spread_kernel, grid=(4,), out_shape=(jax.ShapeDtypeStruct(...  3.72 us

profile of v5, /device:TPU:16, one launch (start us, length us, event | category | flops | bytes accessed | tf_op | source)
XLA Modules:
  0.0 104.7 jit_solution(16674063747881483903)
XLA Ops:
  0.6 100.4 %train_step.1.gathered = s16[2,4,4,144,128]{4,3,2,1,0:T(8,128)(2,1)} custom-call(s32[16,3072]{1,0:T(8,128)} %bitcast.8, s32[1,3072]{1,0:T(1,128)} %bag_hbm.1, bf16[256,128]{1,0:T(8,128)(2,1)} %bitcast.9, bf16[128,4096]{1,0:T(8,128)(2,1)} %w_in.1, f32[32,128]{1,0:T(8,128)} %bitcast.10, f32[1,256]{1,0:T(1,128)} %bitcast.11), custom_call_target="tpu_custom_call" | custom-call | tf_op jit(solution)/shard_map/train_step/pallas_call | solution.py:537
  101.0 3.7 %spread.1 = (f32[128,4096]{1,0:T(8,128)}, f32[256,128]{1,0:T(8,128)}, f32[32,128]{1,0:T(8,128)}) custom-call(s16[2,4,4,144,128]{4,3,2,1,0:T(8,128)(2,1)} %train_step.1.gathered), custom_call_target="tpu_custom_call" | custom-call | tf_op jit(solution)/shard_map/spread/pallas_call | solution.py:566

commit v6 on v5

--- a/solution.py
+++ b/solution.py
@@ -47,7 +47,7 @@
 
 
 def step_kernel(
-    codes_hbm, bag_hbm, book_hbm, w_in, w_out_hbm, labels_hbm, out,
+    codes_hbm, bag_hbm, book_hbm, w_in, w_out_hbm, labels_hbm, out_hbm, out,
     codes, bag, book, w_out, labels, table_t, members, pooled, low, high,
     w_cols, w_turned, fields, fields32, turned, logits, heads,
     gp_own, gp_sib, gp_got, gp_out, gp_in, gq_out, gq_in, gp_sum,
@@ -55,7 +55,7 @@
     table, tab, tab_y, tab_near, tab_far,
     local, w_s, w_r, wu_s, wu_r, wd_s, wd_r, f_s, f_r, sib_s, sib_r, lg_s, lg_r, hd_s, hd_r, gs_s, gs_r, gp_s, gp_r, gq_s, gq_r,
     y_s, y_r, n_s, n_r, fr_s, fr_r, a_s, a_r,
-    ty_s, ty_r, tn_s, tn_r, tf_s, tf_r, of_s, of_r, on_s, on_r, oy_s, oy_r,
+    ty_s, ty_r, tn_s, tn_r, tf_s, tf_r, of_s, of_r, on_s, on_r, oy_s, oy_r, kept,
 ):
     e = lax.axis_index("emb")
     g = lax.axis_index("dense")
@@ -123,6 +123,14 @@
         w_copy(i).wait_recv()
         up_copy(i, own_lanes).start()
         down_copy(i, own_lanes).start()
+
+    pl.semaphore_wait(barrier, EMB - 1 + 8)
+    loop(1, EMB, lambda i: w_copy(i).start())
+    sent.append(lambda: loop(1, EMB, lambda i: w_copy(i).wait_send()))
+    own_w = pltpu.make_async_copy(
+        w_in.at[:, pl.ds(pl.multiple_of(e * WIDE, WIDE), WIDE)], w_cols.at[e], local.at[0]
+    )
+    own_w.start()
 
     def rows_of(f, h):
         return fields.at[f, pl.ds(h * 64, 64)]
@@ -172,13 +180,6 @@
         sent.append(lambda: loop(0, 8, lambda i: sib_copy(i, h).wait_send()))
 
     loop(0, 1, count_step)
-    pl.semaphore_wait(barrier, EMB - 1 + 8)
-    loop(1, EMB, lambda i: w_copy(i).start())
-    sent.append(lambda: loop(1, EMB, lambda i: w_copy(i).wait_send()))
-    own_w = pltpu.make_async_copy(
-        w_in.at[:, pl.ds(pl.multiple_of(e * WIDE, WIDE), WIDE)], w_cols.at[e], local.at[0]
-    )
-    own_w.start()
 
     def later_step(step):
         count_step(step)
@@ -477,9 +478,17 @@
     for m in turns:
         on_wait(2, m)
         put(oy_copy(3, m))
-    for m in range(4):
-        for k in range(4):
+    def keep_all(yy, c, n):
+        pltpu.make_async_copy(out.at[yy, c], out_hbm.at[yy, c], kept.at[n, 0]).start()
+        sent.append(lambda: pltpu.make_async_copy(out.at[yy, c], out_hbm.at[yy, c], kept.at[n, 0]).wait())
+
+    for c in range(4):
+        keep_all(y, c, c)
+    for k in range(4):
+        for m in range(4):
             oy_wait(k, m)
+        off = 0 if k == 0 else ways[k - 1]
+        keep_all(other, lax.rem(z + ZED - off, 4), 4 + k)
     for wait in sent:
         wait()
 
@@ -489,6 +498,7 @@
     V, D = pltpu.VMEM, pltpu.SemaphoreType.DMA
     rows = codes.shape[1]
     scratch = [
+        V((2, 4, 4, BLOCK, 128), I16),
         V((SUB, rows), jnp.int32),
         V((1, rows), jnp.int32),
         V((CENT, D_FIELD), BF16),
@@ -534,11 +544,12 @@
     sems = [(16,), (16,), (16,), (2, 8), (2, 8), (16,), (16,), (8,), (3,), (), (4,), (3,), (3,), (16,), (), (3,), (3,), (3,), (3, 4), (4, 4)]
     for shape in sems:
         scratch += [D(shape), D(shape)] if shape else [D, D]
+    scratch += [D((8, 1))]
     return pl.pallas_call(
         step_kernel,
         out_shape=jax.ShapeDtypeStruct((2, 4, 4, BLOCK, 128), I16),
         in_specs=[hbm] * 6,
-        out_specs=pl.BlockSpec(memory_space=pltpu.VMEM),
+        out_specs=hbm,
         scratch_shapes=scratch,
         compiler_params=pltpu.CompilerParams(
             collective_id=1, has_side_effects=True, vmem_limit_bytes=56 << 20
@@ -547,36 +558,52 @@
     )(codes, bag, book, w_in, w_out, labels)
 
 
-def spread_kernel(gathered, weight, table, head):
-    a = pl.program_id(0)
-    for c in range(4):
-        for yy in range(2):
-            tail = number(gathered[yy, c, 0, 128:])
-            scales = jnp.exp2(tail[8:] - 15.0)
-            whole = number(gathered[yy, c, 0, :128]) * scales[1:2]
-            for f in range(EMB):
-                spot = f * WIDE + yy * 128
-                weight[c * 8 : c * 8 + 8, spot : spot + 128] = whole[f * 8 : f * 8 + 8]
-            gg = yy * ZED + a * 4 + c
-            table[pl.ds(pl.multiple_of(gg * 8, 8), 8), :] = tail[:8] * scales[2:3]
-            head[pl.ds(gg, 1), :] = tail[8:9] * scales[3:4]
+def spread_kernel(gathered, weight, table, head, parts, rows, load_s, store_s):
+    def load(a):
+        return pltpu.make_async_copy(gathered.at[:, :, a], parts.at[a], load_s.at[a])
+
+    def store(a):
+        return pltpu.make_async_copy(rows.at[a], weight.at[pl.ds(a * 32, 32)], store_s.at[a])
+
+    for a in range(4):
+        load(a).start()
+    for a in range(4):
+        load(a).wait()
+        for c in range(4):
+            for yy in range(2):
+                tail = number(parts[a, yy, c, 128:])
+                scales = jnp.exp2(tail[8:] - 15.0)
+                whole = number(parts[a, yy, c, :128]) * scales[1:2]
+                for f in range(EMB):
+                    spot = f * WIDE + yy * 128
+                    rows[a, c * 8 : c * 8 + 8, spot : spot + 128] = whole[f * 8 : f * 8 + 8]
+                gg = yy * ZED + a * 4 + c
+                table[gg * 8 : gg * 8 + 8, :] = tail[:8] * scales[2:3]
+                head[gg : gg + 1, :] = tail[8:9] * scales[3:4]
+        store(a).start()
+    for a in range(4):
+        store(a).wait()
 
 
 def spread(gathered):
+    hbm = pl.BlockSpec(memory_space=pl.ANY)
+    vmem = pl.BlockSpec(memory_space=pltpu.VMEM)
     return pl.pallas_call(
         spread_kernel,
-        grid=(4,),
         out_shape=(
             jax.ShapeDtypeStruct((D_FIELD, HID), F32),
             jax.ShapeDtypeStruct((CENT, D_FIELD), F32),
             jax.ShapeDtypeStruct((DENSE, 128), F32),
         ),
-        in_specs=[pl.BlockSpec((2, 4, 1, BLOCK, 128), lambda i: (0, 0, i, 0, 0))],
-        out_specs=(
-            pl.BlockSpec((32, HID), lambda i: (i, 0)),
-            pl.BlockSpec((CENT, D_FIELD), lambda i: (0, 0)),
-            pl.BlockSpec((DENSE, 128), lambda i: (0, 0)),
-        ),
+        in_specs=[hbm],
+        out_specs=(hbm, vmem, vmem),
+        scratch_shapes=[
+            pltpu.VMEM((4, 2, 4, BLOCK, 128), I16),
+            pltpu.VMEM((4, 32, HID), F32),
+            pltpu.SemaphoreType.DMA((4,)),
+            pltpu.SemaphoreType.DMA((4,)),
+        ],
+        compiler_params=pltpu.CompilerParams(vmem_limit_bytes=60 << 20),
         name="spread",
     )(gathered)
 

time: 105 us -> 104 us (level)
  no operation moved by 1% of the time
where the time goes in v6:
time: 104 us
  Pallas kernels  103 us (99%)
    pallas_call x1, Pallas kernels, train(): pl.pallas_call(step_kernel, out_shape=jax.ShapeDtypeStruct((2, 4, 4, BLOC...  99.8 us
    pallas_call x1, Pallas kernels, spread(): pl.pallas_call(spread_kernel, out_shape=(jax.ShapeDtypeStruct((D_FIELD, H...  3.06 us

profile of v6, /device:TPU:16, one launch (start us, length us, event | category | flops | bytes accessed | tf_op | source)
XLA Modules:
  0.0 103.5 jit_solution(11045810105308756716)
XLA Ops:
  0.6 99.8 %train_step.1.gathered = s16[2,4,4,144,128]{4,3,2,1,0:T(8,128)(2,1)} custom-call(s32[16,3072]{1,0:T(8,128)} %bitcast.8, s32[1,3072]{1,0:T(1,128)} %bag_hbm.1, bf16[256,128]{1,0:T(8,128)(2,1)} %bitcast.9, bf16[128,4096]{1,0:T(8,128)(2,1)} %w_in.1, f32[32,128]{1,0:T(8,128)} %bitcast.10, f32[1,256]{1,0:T(1,128)} %bitcast.11), custom_call_target="tpu_custom_call" | custom-call | tf_op jit(solution)/shard_map/train_step/pallas_call | solution.py:548
  100.5 3.1 %spread.1 = (f32[128,4096]{1,0:T(8,128)}, f32[256,128]{1,0:T(8,128)}, f32[32,128]{1,0:T(8,128)}) custom-call(s16[2,4,4,144,128]{4,3,2,1,0:T(8,128)(2,1)} %train_step.1.gathered), custom_call_target="tpu_custom_call" | custom-call | tf_op jit(solution)/shard_map/spread/pallas_call | solution.py:591

commit v7 on v6

--- a/solution.py
+++ b/solution.py
@@ -51,10 +51,10 @@
     codes, bag, book, w_out, labels, table_t, members, pooled, low, high,
     w_cols, w_turned, fields, fields32, turned, logits, heads,
     gp_own, gp_sib, gp_got, gp_out, gp_in, gq_out, gq_in, gp_sum,
-    y_out, y_in, mine, near_out, near_in, acc, far_out, far_in, red, cols,
+    y_out, y_in, mine, near_out, near_in, two_out, two_in, acc, far_out, far_in, red, cols,
     table, tab, tab_y, tab_near, tab_far,
     local, w_s, w_r, wu_s, wu_r, wd_s, wd_r, f_s, f_r, sib_s, sib_r, lg_s, lg_r, hd_s, hd_r, gs_s, gs_r, gp_s, gp_r, gq_s, gq_r,
-    y_s, y_r, n_s, n_r, fr_s, fr_r, a_s, a_r,
+    y_s, y_r, n_s, n_r, two_s, two_r, fr_s, fr_r, a_s, a_r,
     ty_s, ty_r, tn_s, tn_r, tf_s, tf_r, of_s, of_r, on_s, on_r, oy_s, oy_r, kept,
 ):
     e = lax.axis_index("emb")
@@ -311,16 +311,28 @@
         mine[c] = grad_half(c, y)
 
     def near_copy(k):
-        return send(near_out.at[k], near_in.at[k], n_s.at[k], n_r.at[k], z_at(near[k]))
+        return send(near_out.at[k - 1], near_in.at[k - 1], n_s.at[k - 1], n_r.at[k - 1], z_at(near[k]))
+
+    def two_copy(h):
+        return send(two_out.at[h], two_in.at[h], two_s.at[h], two_r.at[h], z_at(2 - 4 * h))
 
     for k in range(3):
         c = order[k]
         y_copy(k, c).wait_recv()
-        coded, power = encode(mine[c] + decode(y_in[c, :512], y_in[c, 512:]))
-        near_out[k, :512] = coded
-        near_out[k, 512:] = tile_of(power)
-        near_copy(k).start()
-        sent.append(lambda k=k: near_copy(k).wait_send())
+        pair = mine[c] + decode(y_in[c, :512], y_in[c, 512:])
+        if k == 0:
+            for h in range(2):
+                coded, power = encode(pair[h * 256 : h * 256 + 256])
+                two_out[h, :256] = coded
+                two_out[h, 256:] = tile_of(power)
+                two_copy(h).start()
+                sent.append(lambda h=h: two_copy(h).wait_send())
+        else:
+            coded, power = encode(pair)
+            near_out[k - 1, :512] = coded
+            near_out[k - 1, 512:] = tile_of(power)
+            near_copy(k).start()
+            sent.append(lambda k=k: near_copy(k).wait_send())
     y_copy(3, zr).wait_recv()
     acc[...] = (mine[zr] + decode(y_in[zr, :512], y_in[zr, 512:])).reshape(4, 128, 128)
 
@@ -340,9 +352,13 @@
     sent.append(lambda: gq_copy.wait_send())
     gp_sum[...] = row_sum(y_high)
 
-    for k in range(3):
+    for h in range(2):
+        two_copy(h).wait_recv()
+        two = slice(h * 2, h * 2 + 2)
+        acc[two] = acc[two] + decode(two_in[h, :256], two_in[h, 256:]).reshape(2, 128, 128)
+    for k in (1, 2):
         near_copy(k).wait_recv()
-        acc[...] = acc[...] + decode(near_in[k, :512], near_in[k, 512:]).reshape(4, 128, 128)
+        acc[...] = acc[...] + decode(near_in[k - 1, :512], near_in[k - 1, 512:]).reshape(4, 128, 128)
 
     def far_copy(m):
         return send(far_out.at[m - 1], far_in.at[m - 1], fr_s.at[m - 1], fr_r.at[m - 1], z_at(4 * m))
@@ -440,19 +456,32 @@
     ways = (1, -1, 2)
 
     def on_copy(k, m):
-        got = block(1 if k == 2 else 0, m)
-        return send(got, got, on_s.at[k, m], on_r.at[k, m], z_at(-1 if k == 1 else 1))
+        return send(block(0, m), block(0, m), on_s.at[k, m], on_r.at[k, m], z_at(ways[k]))
 
     def on_wait(k, m):
         got = block(ways[k], m)
-        send(got, got, on_s.at[k, m], on_r.at[k, m], z_at(1)).wait_recv()
+        send(got, got, on_s.at[k, m], on_r.at[k, m], z_at(ways[k])).wait_recv()
+
+    chain = ((1, 0), (1, 1), (-1, 0), (-1, 3))
+
+    def ch_copy(i):
+        way, m = chain[i]
+        return send(block(way, m), block(way, m), on_s.at[2, i], on_r.at[2, i], z_at(way))
+
+    def ch_block(i):
+        way, m = chain[i]
+        return block(2 * way, m)
+
+    def ch_wait(i):
+        send(ch_block(i), ch_block(i), on_s.at[2, i], on_r.at[2, i], z_at(chain[i][0])).wait_recv()
 
     def oy_copy(k, m):
-        got = block(0 if k == 0 else ways[k - 1], m)
+        got = ch_block(m) if k == 3 else block(0 if k == 0 else ways[k - 1], m)
         return send(got, got, oy_s.at[k, m], oy_r.at[k, m], y_mate)
 
     def oy_wait(k, m):
-        src = lax.rem(z + 2 * ZED - (0 if k == 0 else ways[k - 1]) - 4 * m, ZED)
+        off, at = (2 * chain[m][0], chain[m][1]) if k == 3 else (0 if k == 0 else ways[k - 1], m)
+        src = lax.rem(z + 2 * ZED - off - 4 * at, ZED)
         got = out.at[other, lax.rem(src, 4), src // 4]
         send(got, got, oy_s.at[k, m], oy_r.at[k, m], y_mate).wait_recv()
 
@@ -471,13 +500,16 @@
         put(oy_copy(0, m))
     for m in turns:
         on_wait(0, m)
-        put(on_copy(2, m))
+        if (1, m) in chain:
+            put(ch_copy(chain.index((1, m))))
         put(oy_copy(1, m))
         on_wait(1, m)
+        if (-1, m) in chain:
+            put(ch_copy(chain.index((-1, m))))
         put(oy_copy(2, m))
-    for m in turns:
-        on_wait(2, m)
-        put(oy_copy(3, m))
+    for i in (0, 2, 1, 3):
+        ch_wait(i)
+        put(oy_copy(3, i))
     def keep_all(yy, c, n):
         pltpu.make_async_copy(out.at[yy, c], out_hbm.at[yy, c], kept.at[n, 0]).start()
         sent.append(lambda: pltpu.make_async_copy(out.at[yy, c], out_hbm.at[yy, c], kept.at[n, 0]).wait())
@@ -527,8 +559,10 @@
         V((4, 528, 128), I16),
         V((4, 528, 128), I16),
         V((4, 512, 128), F32),
-        V((3, 528, 128), I16),
-        V((3, 528, 128), I16),
+        V((2, 528, 128), I16),
+        V((2, 528, 128), I16),
+        V((2, 272, 128), I16),
+        V((2, 272, 128), I16),
         V((4, 128, 128), F32),
         V((3, 144, 128), I16),
         V((3, 144, 128), I16),
@@ -541,7 +575,7 @@
         V((3, 16, 128), F32),
         D((6,)),
     ]
-    sems = [(16,), (16,), (16,), (2, 8), (2, 8), (16,), (16,), (8,), (3,), (), (4,), (3,), (3,), (16,), (), (3,), (3,), (3,), (3, 4), (4, 4)]
+    sems = [(16,), (16,), (16,), (2, 8), (2, 8), (16,), (16,), (8,), (3,), (), (4,), (2,), (2,), (3,), (16,), (), (3,), (3,), (3,), (3, 4), (4, 4)]
     for shape in sems:
         scratch += [D(shape), D(shape)] if shape else [D, D]
     scratch += [D((8, 1))]

time: 104 us -> 104 us (level)
  the two profiles are of different devices: /device:TPU:16 before, /device:TPU:6 now
where the time goes in v7:
time: 104 us; the launch traced here: 103 us
  Pallas kernels  102 us (98%)
    pallas_call x1, Pallas kernels, train(): pl.pallas_call(step_kernel, out_shape=jax.ShapeDtypeStruct((2, 4, 4, BLOC...  99.4 us
    pallas_call x1, Pallas kernels, spread(): pl.pallas_call(spread_kernel, out_shape=(jax.ShapeDtypeStruct((D_FIELD, H...  3.06 us

profile of v7, /device:TPU:6, one launch (start us, length us, event | category | flops | bytes accessed | tf_op | source)
XLA Modules:
  0.0 103.1 jit_solution(16225559917426090641)
XLA Ops:
  0.6 99.4 %train_step.1.gathered = s16[2,4,4,144,128]{4,3,2,1,0:T(8,128)(2,1)} custom-call(s32[16,3072]{1,0:T(8,128)} %bitcast.8, s32[1,3072]{1,0:T(1,128)} %bag_hbm.1, bf16[256,128]{1,0:T(8,128)(2,1)} %bitcast.9, bf16[128,4096]{1,0:T(8,128)(2,1)} %w_in.1, f32[32,128]{1,0:T(8,128)} %bitcast.10, f32[1,256]{1,0:T(1,128)} %bitcast.11), custom_call_target="tpu_custom_call" | custom-call | tf_op jit(solution)/shard_map/train_step/pallas_call | solution.py:582
  100.0 3.1 %spread.1 = (f32[128,4096]{1,0:T(8,128)}, f32[256,128]{1,0:T(8,128)}, f32[32,128]{1,0:T(8,128)}) custom-call(s16[2,4,4,144,128]{4,3,2,1,0:T(8,128)(2,1)} %train_step.1.gathered), custom_call_target="tpu_custom_call" | custom-call | tf_op jit(solution)/shard_map/spread/pallas_call | solution.py:625

commit v8 on v6

--- a/solution.py
+++ b/solution.py
@@ -261,15 +261,6 @@
         y_out[c, 512:] = tile_of(power)
         y_copy(k, c).start()
         sent.append(lambda k=k, c=c: y_copy(k, c).wait_send())
-    head = lax.dot_general(slope, act, NT, precision=lax.Precision.HIGHEST, preferred_element_type=F32)
-    heads[e] = jnp.concatenate([head[:1, :128], head[:1, 128:], jnp.zeros((6, 128), F32)], axis=0)
-
-    def hd_copy(i):
-        return send(heads.at[e], heads.at[e], hd_s.at[i], hd_r.at[i], (emb_at(i), g))
-
-    loop(1, EMB, lambda i: hd_copy(i).start())
-    sent.append(lambda: loop(1, EMB, lambda i: hd_copy(i).wait_send()))
-
     core = lax.rem(e, 2)
 
     def gs_copy(i):
@@ -307,6 +298,15 @@
     sent.append(lambda: loop(1, 4, lambda i: gp_copy(i).wait_send()))
     for h in range(2):
         gs_copy(h * 4 + col).wait_recv()
+    head = lax.dot_general(slope, act, NT, precision=lax.Precision.HIGHEST, preferred_element_type=F32)
+    heads[e] = jnp.concatenate([head[:1, :128], head[:1, 128:], jnp.zeros((6, 128), F32)], axis=0)
+
+    def hd_copy(i):
+        return send(heads.at[e], heads.at[e], hd_s.at[i], hd_r.at[i], (emb_at(i), g))
+
+    loop(1, EMB, lambda i: hd_copy(i).start())
+    sent.append(lambda: loop(1, EMB, lambda i: hd_copy(i).wait_send()))
+
     for k, c in enumerate(order):
         mine[c] = grad_half(c, y)
 

time: 104 us -> 104 us (level)
  no operation moved by 1% of the time
where the time goes in v8:
time: 104 us
  Pallas kernels  103 us (99%)
    pallas_call x1, Pallas kernels, train(): pl.pallas_call(step_kernel, out_shape=jax.ShapeDtypeStruct((2, 4, 4, BLOC...  99.9 us
    pallas_call x1, Pallas kernels, spread(): pl.pallas_call(spread_kernel, out_shape=(jax.ShapeDtypeStruct((D_FIELD, H...  3.06 us

profile of v8, /device:TPU:16, one launch (start us, length us, event | category | flops | bytes accessed | tf_op | source)
XLA Modules:
  0.0 103.6 jit_solution(9436238995050599038)
XLA Ops:
  0.6 99.9 %train_step.1.gathered = s16[2,4,4,144,128]{4,3,2,1,0:T(8,128)(2,1)} custom-call(s32[16,3072]{1,0:T(8,128)} %bitcast.8, s32[1,3072]{1,0:T(1,128)} %bag_hbm.1, bf16[256,128]{1,0:T(8,128)(2,1)} %bitcast.9, bf16[128,4096]{1,0:T(8,128)(2,1)} %w_in.1, f32[32,128]{1,0:T(8,128)} %bitcast.10, f32[1,256]{1,0:T(1,128)} %bitcast.11), custom_call_target="tpu_custom_call" | custom-call | tf_op jit(solution)/shard_map/train_step/pallas_call | solution.py:548
  100.5 3.1 %spread.1 = (f32[128,4096]{1,0:T(8,128)}, f32[256,128]{1,0:T(8,128)}, f32[32,128]{1,0:T(8,128)}) custom-call(s16[2,4,4,144,128]{4,3,2,1,0:T(8,128)(2,1)} %train_step.1.gathered), custom_call_target="tpu_custom_call" | custom-call | tf_op jit(solution)/shard_map/spread/pallas_call | solution.py:591
